TPU v7x, 256 devices: a whole 4x4x8 slice. The times are simulated.
256 devices in a mesh: row: 32 (over z, y_lo, core), col: 8 (over y_hi, x).
Axes of the slice: x: 4, y: 4 (y_hi: 2, y_lo: 2; y = y_hi * 2 + y_lo), z: 8, core: 2. Of those that a mesh axis runs over, the one named last changes fastest.
Arguments:
- features: bfloat16 [131072, 128], P(('row', 'col')), may hold values from -6 to 6
- self_weight: bfloat16 [128, 256], replicated, may hold values from -0.5 to 0.5
- neigh_weight: bfloat16 [128, 256], replicated, may hold values from -0.5 to 0.5
- block_row: int32 [32, 8, 512], P('row', 'col'), may hold values from 0 to 63, as said below
- block_col: int32 [32, 8, 512], P('row', 'col'), may hold values from 0 to 255
- block_count: int32 [32, 8], P('row', 'col'), may hold values from 64 to 512, as said below
- edge_weight: int32 [32, 8, 512, 4096], P('row', 'col'), may hold values from 0 to 1, as said below
- train_mask: int32 [131072], P(('row', 'col')), may hold values 0 or 1
- out_cotangent: bfloat16 [131072, 256], P(('row', 'col')), may hold values from -6 to 6
Outputs:
- hidden: bfloat16 [131072, 256], P(('row', 'col'))
- grad_input: bfloat16 [131072, 128], P(('row', 'col'))
- grad_self: float32 [128, 256], replicated
- grad_neigh: float32 [128, 256], replicated
Inputs may be any that keep to these rules, and one draw needn't show every extreme that they name: block_row is s for every slot s < 64, so every block row of every tile holds a live block. `block_count`: one tile in every draw has exactly 512 live slots. `edge_weight`: in every slot s < 64 the block's diagonal entries are 1.
All inputs are finite; a program needn't handle non-finite values. No bound on the sum of `train_mask` on one device may be relied on, other than what follows from the above.
Results may differ from a plain program's by a relative error of at most 0.019.
Values may be sent and summed in bfloat16 or wider, within the bound.
A program may use at most 128 MiB of HBM per device.

v0:
```python
import jax
import jax.numpy as jnp
from jax import lax
from jax.sharding import PartitionSpec as P

BLOCK = 64


def forward_slots(gathered, rows_in, cols_in, wts_int, valid, tile_rows):
    width = gathered.shape[1]
    blocks = gathered.reshape(-1, BLOCK, width)[cols_in]
    live = wts_int.reshape(-1, BLOCK, BLOCK) * valid[:, None, None]
    wmat = live.astype(jnp.bfloat16)
    prod = jnp.einsum("sab,sbd->sad", wmat, blocks, preferred_element_type=jnp.float32)
    partial_value = jax.ops.segment_sum(prod, rows_in, num_segments=tile_rows // BLOCK)
    degrees = jax.ops.segment_sum(
        jnp.sum(live, axis=2).astype(jnp.float32), rows_in, num_segments=tile_rows // BLOCK
    )
    return (partial_value.reshape(tile_rows, width), degrees.reshape(tile_rows))


def backward_slots(gathered, rows_in, cols_in, wts_int, valid, tile_cols):
    width = gathered.shape[1]
    blocks = gathered.reshape(-1, BLOCK, width)[rows_in]
    wmat = (wts_int.reshape(-1, BLOCK, BLOCK) * valid[:, None, None]).astype(jnp.bfloat16)
    contrib = jnp.einsum("sab,sad->sbd", wmat, blocks, preferred_element_type=jnp.float32)
    return jax.ops.segment_sum(contrib, cols_in, num_segments=tile_cols // BLOCK).reshape(
        tile_cols, width
    )


def shards(
    features,
    self_weight,
    neigh_weight,
    block_row,
    block_col,
    block_count,
    edge_weight,
    train_mask,
    out_cotangent,
):
    owned = features.shape[0]
    tile_rows = lax.axis_size("col") * owned
    tile_cols = lax.axis_size("row") * owned
    rows_in = block_row[0, 0]
    cols_in = block_col[0, 0]
    count = block_count[0, 0]
    wts_int = edge_weight[0, 0]
    valid = (jnp.arange(rows_in.shape[0]) < count).astype(jnp.int32)
    gathered = lax.all_gather(features, "row", axis=0, tiled=True)
    partial_value, degree_part = forward_slots(
        gathered, rows_in, cols_in, wts_int, valid, tile_rows
    )
    raw, degree = (
        lax.psum_scatter(
            partial_value.astype(jnp.bfloat16), "col", scatter_dimension=0, tiled=True
        ).astype(jnp.float32),
        lax.psum_scatter(
            degree_part.astype(jnp.bfloat16), "col", scatter_dimension=0, tiled=True
        ).astype(jnp.float32),
    )
    agg = (raw / degree[:, None]).astype(jnp.bfloat16)
    pre = jnp.dot(features, self_weight, preferred_element_type=jnp.float32) + jnp.dot(
        agg, neigh_weight, preferred_element_type=jnp.float32
    )
    hidden = jax.nn.silu(pre).astype(jnp.bfloat16)
    sig = jax.nn.sigmoid(pre)
    dpre = (
        out_cotangent.astype(jnp.float32)
        * train_mask.astype(jnp.float32)[:, None]
        * sig
        * (1.0 + pre * (1.0 - sig))
    ).astype(jnp.bfloat16)
    contract_rows = (((0,), (0,)), ((), ()))
    contract_cols = (((1,), (1,)), ((), ()))
    grad_self_part = lax.dot_general(
        features, dpre, contract_rows, preferred_element_type=jnp.float32
    )
    grad_neigh_part = lax.dot_general(agg, dpre, contract_rows, preferred_element_type=jnp.float32)
    grad_self, grad_neigh = lax.psum((grad_self_part, grad_neigh_part), ("row", "col"))
    scaled = (
        lax.dot_general(dpre, neigh_weight, contract_cols, preferred_element_type=jnp.float32)
        / degree[:, None]
    ).astype(jnp.bfloat16)
    scaled_group = lax.all_gather(scaled, "col", axis=0, tiled=True)
    transposed = backward_slots(scaled_group, rows_in, cols_in, wts_int, valid, tile_cols)
    through = lax.psum_scatter(
        transposed.astype(jnp.bfloat16), "row", scatter_dimension=0, tiled=True
    ).astype(jnp.float32)
    own_term = lax.dot_general(dpre, self_weight, contract_cols, preferred_element_type=jnp.float32)
    grad_input = (own_term + through).astype(jnp.bfloat16)
    return (hidden, grad_input, grad_self, grad_neigh)


def solution(mesh):
    in_specs = (
        P(("row", "col"), None),
        P(),
        P(),
        P("row", "col", None),
        P("row", "col", None),
        P("row", "col"),
        P("row", "col", None, None),
        P(("row", "col")),
        P(("row", "col"), None),
    )
    out_specs = (P(("row", "col"), None), P(("row", "col"), None), P(), P())
    return jax.shard_map(shards, mesh=mesh, in_specs=in_specs, out_specs=out_specs, check_vma=False)
```

profile of v0, /device:TPU:1, one launch (start us, length us, event | category | flops | bytes accessed | tf_op | source)
XLA Modules:
  0.0 689.2 jit_solution(6560467520446752218)
XLA Ops:
  8.0 9.0 %copy.24 = s32[1,1,512,4096]{2,3,1,0:T(8,128)} copy(s32[1,1,512,4096]{3,2,1,0:T(8,128)} %param.15) | data formatting | bytes 16777216 | tf_op args[6]
  17.6 7.4 %multiply_reduce_fusion = (s32[512,64]{0,1:T(8,128)S(1)}, bf16[512,64,64]{0,2,1:T(8,128)(2,1)}) fusion(s32[512,64,64]{0,2,1:T(8,128)} %bitcast.33, s32[512]{0:T(512)S(1)} %fusion.4), kind=kLoop, calls=%fused_computation.5 | loop fusion | flops 6258688 | bytes 12716032 | tf_op jit(solution)/shard_map/reduce_sum | solution.py:17
  25.0 15.7 %copy.27 = bf16[512,64,64]{1,2,0:T(8,128)(2,1)} copy(bf16[512,64,64]{0,2,1:T(8,128)(2,1)} %get-tuple-element.23) | data formatting | bytes 8388608 | tf_op jit(solution)/shard_map/convert_element_type | solution.py:13
  40.7 40.2 %all-gather.3.cloned.1.call-done = bf16[16384,128]{1,0:T(8,128)(2,1)} async-done(((bf16[512,128]{1,0:T(8,128)(2,1)}), bf16[16384,128]{1,0:T(8,128)(2,1)}) %all-gather.3.cloned.1.call-update) | async-done | bytes 4194320 | tf_op jit(solution)/shard_map/all_gather | solution.py:51
  80.9 22.0 %gather_fusion = bf16[512,64,128]{2,1,0:T(8,128)(2,1)} fusion(bf16[256,64,128]{2,1,0:T(8,128)(2,1)} %bitcast.35, s32[1024]{0:T(1024)S(1)} %pad_clamp_fusion.1), kind=kCustom, calls=%fused_computation | custom fusion | bytes 16779264 | tf_op jit(solution)/shard_map/gather | solution.py:11
  103.0 14.4 %fusion.7 = f32[512,64,128]{2,1,0:T(8,128)} fusion(bf16[512,64,64]{1,2,0:T(8,128)(2,1)} %copy.27, bf16[512,64,128]{2,1,0:T(8,128)(2,1)} %gather_fusion), kind=kOutput, calls=%fused_computation.28 | convolution fusion | flops 536870912 | bytes 29360128 | tf_op jit(solution)/shard_map/sab,sbd->sad/dot_general | solution.py:14
  117.7 51.8 %scatter_fusion = f32[64,64,128]{2,1,0:T(8,128)S(1)} fusion(f32[64,64,128]{2,1,0:T(8,128)S(1)} %broadcast_in_dim.6, s32[512]{0:T(512)S(1)} %bitcast.37, f32[512,64,128]{2,1,0:T(8,128)} %fusion.7), kind=kCustom, calls=%fused_computation.2 | custom fusion | flops 4194304 | bytes 50333696 | tf_op jit(solution)/shard_map/scatter-add | solution.py:15
  169.5 1.2 convert_element_type.64
  170.9 2.3 scatter_custom_fusion.1
  174.5 20.4 %all-reduce = bf16[4096]{0:T(1024)(128)(2,1)S(1)} all-reduce(bf16[4096]{0:T(1024)(128)(2,1)S(1)} %convert_element_type.69), channel_id=3, replica_groups=mesh['row'=32,'col'=8] {'col'}, use_global_device_ids=true, to_apply=%region_4.0.clone | all-reduce | flops 4096 | bytes 16384
  195.3 50.2 %reduce-scatter.3.cloned.1.call-done = bf16[512,128]{1,0:T(8,128)(2,1)} async-done(((bf16[4096,128]{1,0:T(8,128)(2,1)}), bf16[512,128]{1,0:T(8,128)(2,1)}) %reduce-scatter.3.cloned.1.call-update) | async-done | bytes 131088 | tf_op jit(solution)/shard_map/reduce_scatter | solution.py:56
  245.5 2.0 multiply_convert_fusion.1
  249.5 1.9 fusion.5
  251.4 50.1 %all-gather.5.cloned.1.call-done = bf16[4096,128]{1,0:T(8,128)(2,1)} async-done(((bf16[512,128]{1,0:T(8,128)(2,1)}), bf16[4096,128]{1,0:T(8,128)(2,1)}) %all-gather.5.cloned.1.call-update) | async-done | bytes 1048592 | tf_op jit(solution)/shard_map/all_gather | solution.py:86
  301.6 21.1 %gather_fusion.1 = bf16[512,64,128]{2,1,0:T(8,128)(2,1)} fusion(bf16[64,64,128]{2,1,0:T(8,128)(2,1)} %bitcast.32, s32[1024]{0:T(1024)S(1)} %pad_clamp_fusion), kind=kCustom, calls=%fused_computation.1 | custom fusion | bytes 16779264 | tf_op jit(solution)/shard_map/gather | solution.py:24
  322.7 13.9 %fusion.8 = f32[512,64,128]{2,1,0:T(8,128)} fusion(bf16[512,64,64]{1,2,0:T(8,128)(2,1)} %copy.27, bf16[512,64,128]{2,1,0:T(8,128)(2,1)} %gather_fusion.1), kind=kOutput, calls=%fused_computation.29 | convolution fusion | flops 536870912 | bytes 29360128 | tf_op jit(solution)/shard_map/sab,sad->sbd/dot_general | solution.py:26
  336.5 4.3 broadcast_in_dim.8
  340.8 79.3 %scatter_fusion.1 = f32[256,64,128]{2,1,0:T(8,128)} fusion(f32[256,64,128]{2,1,0:T(8,128)} %broadcast_in_dim.8, s32[512]{0:T(512)S(1)} %bitcast.39, f32[512,64,128]{2,1,0:T(8,128)} %fusion.8), kind=kCustom, calls=%fused_computation.4 | custom fusion | flops 4194304 | bytes 50333696 | tf_op jit(solution)/shard_map/scatter-add | solution.py:27
  420.2 6.5 convert_element_type.77
  426.7 130.9 %all-reduce.4.cloned.1.call-done = (f32[128,256]{0,1:T(8,128)}, f32[128,256]{1,0:T(8,128)}) async-done(((f32[128,256]{0,1:T(8,128)}, f32[128,256]{1,0:T(8,128)}), (f32[128,256]{0,1:T(8,128)}, f32[128,256]{1,0:T(8,128)})) %all-reduce.4.cloned.1.call-update) | async-done | bytes 262160 | tf_op jit(solution)/shard_map/psum | solution.py:81
  557.6 1.7 copy.28
  559.2 120.1 %reduce-scatter.5.cloned.1.call-done = bf16[512,128]{1,0:T(8,128)(2,1)} async-done(((bf16[16384,128]{1,0:T(8,128)(2,1)}), bf16[512,128]{1,0:T(8,128)(2,1)}) %reduce-scatter.5.cloned.1.call-update) | async-done | bytes 131088 | tf_op jit(solution)/shard_map/reduce_scatter | solution.py:88
  679.4 1.8 fusion
  681.1 1.6 copy.34
  (44 shorter events, 4.2 us)
Async XLA Ops:
  7.2 238.3 %copy-start = (bf16[128,256]{1,0:T(8,128)(2,1)S(1)}, bf16[128,256]{1,0:T(8,128)(2,1)}, u32[]{:S(2)}) copy-start(bf16[128,256]{1,0:T(8,128)(2,1)} %param.11) | copy-start | bytes 196612
  7.2 73.8 %all-gather.3.cloned.1.call-start = ((), (), s32[]{:S(2)}) async-start(), calls=%async_computation.2 | async-start | bytes 4325376 | tf_op jit(solution)/shard_map/all_gather | solution.py:51
  7.9 237.6 %reduce-scatter.3.cloned.1.call-start = ((), (), s32[]{:S(2)}) async-start(), calls=%async_computation.3 | async-start | bytes 1179648 | tf_op jit(solution)/shard_map/reduce_scatter | solution.py:56
  25.0 15.7 %copy-start.5 = (s32[1,1,512]{2,1,0:T(1,128)S(1)}, s32[1,1,512]{2,1,0:T(1,128)}, u32[]{:S(2)}) copy-start(s32[1,1,512]{2,1,0:T(1,128)} %param.13) | copy-start | bytes 6148
  103.0 14.6 %copy-start.4 = (s32[1,1,512]{2,1,0:T(1,128)S(1)}, s32[1,1,512]{2,1,0:T(1,128)}, u32[]{:S(2)}) copy-start(s32[1,1,512]{2,1,0:T(1,128)} %param.12) | copy-start | bytes 6148
  117.6 55.7 %copy-start.6 = (s32[512]{0:T(512)S(1)}, s32[512]{0:T(512)}, u32[]{:S(2)}) copy-start(s32[512]{0:T(512)} %param.16) | copy-start | bytes 6148
  117.6 55.7 %copy-start.8 = (u32[256]{0:T(256)S(1)}, u32[256]{0:T(256)}, u32[]{:S(2)}) copy-start(u32[256]{0:T(256)} %constant.21) | copy-start | bytes 3076
  117.6 77.4 %copy-start.2 = (bf16[512,128]{1,0:T(8,128)(2,1)S(1)}, bf16[512,128]{1,0:T(8,128)(2,1)}, u32[]{:S(2)}) copy-start(bf16[512,128]{1,0:T(8,128)(2,1)} %param.9) | copy-start | bytes 393220
  117.6 77.4 %copy-start.3 = (bf16[128,256]{1,0:T(8,128)(2,1)S(1)}, bf16[128,256]{1,0:T(8,128)(2,1)}, u32[]{:S(2)}) copy-start(bf16[128,256]{1,0:T(8,128)(2,1)} %param.10) | copy-start | bytes 196612
  117.7 127.8 %copy-start.7 = (bf16[512,256]{1,0:T(8,128)(2,1)S(1)}, bf16[512,256]{1,0:T(8,128)(2,1)}, u32[]{:S(2)}) copy-start(bf16[512,256]{1,0:T(8,128)(2,1)} %param.17) | copy-start | bytes 786436
  170.7 130.9 %all-gather.5.cloned.1.call-start = ((), (), s32[]{:S(2)}) async-start(), calls=%async_computation.4 | async-start | bytes 1179648 | tf_op jit(solution)/shard_map/all_gather | solution.py:86
  248.5 309.1 %all-reduce.4.cloned.1.call-start = ((), (), s32[]{:S(2)}) async-start(), calls=%async_computation.6 | async-start | bytes 524288 | tf_op jit(solution)/shard_map/psum | solution.py:81
  251.4 428.0 %reduce-scatter.5.cloned.1.call-start = ((), (), s32[]{:S(2)}) async-start(), calls=%async_computation.5 | async-start | bytes 4325376 | tf_op jit(solution)/shard_map/reduce_scatter | solution.py:88
  340.8 341.9 %copy-start.1 = (bf16[128,256]{1,0:T(8,128)(2,1)S(1)}, bf16[128,256]{1,0:T(8,128)(2,1)}, u32[]{:S(2)}) copy-start(bf16[128,256]{1,0:T(8,128)(2,1)} %param.11) | copy-start | bytes 196612
Sparse Core Ops, SparseCore 0:
  9.9 71.0 all-gather.2
  170.8 74.6 reduce-scatter.2
  249.0 52.4 all-gather.4
  308.5 248.9 all-reduce.3
  560.1 119.2 reduce-scatter.4
where the time goes:
time: 695 us; the launch traced here: 689 us
  waiting for transfers between devices  392 us (56%)
  other arithmetic  149 us (21%)
  local copies, waits for them, and re-layouts  76.4 us (11%)
  matrix products  36 us (5%)
  blocking collectives  20.4 us (3%)
  between operations  15.3 us (2%)
    psum x1, waiting for transfers between devices, shards(): lax.psum((grad_self_part, grad_neigh_part), ('row', 'col'))  131 us
    reduce_scatter x1, waiting for transfers between devices, shards(): lax.psum_scatter(transposed.astype(jnp.bfloat16), 'row', scatter_dimensio...  120 us
    scatter-add x1, other arithmetic, backward_slots(): jax.ops.segment_sum(contrib, cols_in, num_segments=tile_cols // BLOCK)  79.3 us
    scatter-add x1, other arithmetic, forward_slots(): jax.ops.segment_sum(prod, rows_in, num_segments=tile_rows // BLOCK)  51.8 us
    reduce_scatter x1, waiting for transfers between devices, shards(): lax.psum_scatter(partial_value.astype(jnp.bfloat16), 'col', scatter_dimen...  50.2 us
    all_gather x1, waiting for transfers between devices, shards(): scaled_group = lax.all_gather(scaled, 'col', axis=0, tiled=True)  50.1 us
    all_gather x1, waiting for transfers between devices, shards(): gathered = lax.all_gather(features, 'row', axis=0, tiled=True)  40.2 us
    gather x1, local copies, waits for them, and re-layouts, forward_slots(): blocks = gathered.reshape(-1, BLOCK, width)[cols_in]  22 us
  transfers between devices with their start and end apart: 5, of which 5 were waited for; matrix products, arithmetic and copies ran while one was open for 24% of the time, Pallas kernels for 0%

commit v1 on v0

v1 whole, which is shorter than its diff:
```python
import functools

import jax
import jax.numpy as jnp
from jax import lax
from jax.experimental import pallas as pl
from jax.experimental.pallas import tpu as pltpu
from jax.sharding import PartitionSpec as P

MESH = pl.DeviceIdType.MESH
BF = jnp.bfloat16
F32 = jnp.float32
VMEM = pl.BlockSpec(memory_space=pltpu.VMEM)
SMEM = pl.BlockSpec(memory_space=pltpu.SMEM)
ANY = pl.BlockSpec(memory_space=pl.ANY)
ND = 512
LIMIT = 52 << 20
UNROLL = 16


def place():
    row = lax.axis_index("row")
    return row // 4, (row // 2) % 2, row % 2, lax.axis_index("col")


def greet(targets):
    barrier = pltpu.get_barrier_semaphore()
    for target in targets:
        pl.semaphore_signal(barrier, inc=1, device_id=target, device_id_type=MESH)
    pl.semaphore_wait(barrier, len(targets))


def prep_kernel(cnt, rows, w, zf, zt, deg, pat, dsl):
    i = pl.program_id(0)

    @pl.when(i == 0)
    def _():
        at = lax.broadcasted_iota(jnp.int32, (4096, 128), 0) // 64
        pat[...] = (at == lax.broadcasted_iota(jnp.int32, (4096, 128), 1)).astype(BF)

    lim = cnt[0]
    low = lax.broadcasted_iota(jnp.int32, (32, 128), 1) < 64

    @pl.loop(0, 8)
    def _(g8):
        b = pl.multiple_of(g8 * 8, 8)
        x = w[pl.ds(b, 8), :]
        live = (i * 64 + b + lax.broadcasted_iota(jnp.int32, (8, 4096), 0)) < lim
        y = jnp.where(live, x, 0).astype(F32).reshape(8, 32, 128)
        for h4 in range(2):
            y4 = [y[h4 * 4 + s] for s in range(4)]
            r4 = [pltpu.roll(v, 64, 1) for v in y4]
            z = jnp.concatenate(
                [
                    jnp.where(low, y4[0], r4[2]),
                    jnp.where(low, r4[0], y4[2]),
                    jnp.where(low, y4[1], r4[3]),
                    jnp.where(low, r4[1], y4[3]),
                ],
                0,
            )
            zf[g8 * 2 + h4] = z.astype(BF)
            zt[g8 * 2 + h4] = z.T.astype(BF)

    live = (i * 64 + lax.broadcasted_iota(jnp.int32, (64, 4096), 0)) < lim
    xb = jnp.where(live, w[...], 0).astype(F32).astype(BF)
    dsl[pl.ds(pl.multiple_of(i * 64, 64), 64), :] = jnp.dot(
        xb, pat[...], preferred_element_type=F32
    ).astype(BF)

    @pl.when(i == 7)
    def _():
        hot = (lax.broadcasted_iota(jnp.int32, (64, 512), 0) == rows[...]).astype(F32).astype(BF)
        deg[...] = jnp.dot(hot, dsl[...], preferred_element_type=F32)


def prep(count, rows, w):
    return pl.pallas_call(
        prep_kernel,
        grid=(8,),
        in_specs=[
            SMEM,
            pl.BlockSpec((1, 512), lambda i: (0, 0)),
            pl.BlockSpec((64, 4096), lambda i: (i, 0)),
        ],
        out_specs=[
            pl.BlockSpec((16, 128, 128), lambda i: (i, 0, 0)),
            pl.BlockSpec((16, 128, 128), lambda i: (i, 0, 0)),
            pl.BlockSpec((64, 128), lambda i: (0, 0)),
        ],
        out_shape=[jax.ShapeDtypeStruct((128, 128, 128), BF)] * 2
        + [jax.ShapeDtypeStruct((64, 128), F32)],
        scratch_shapes=[pltpu.VMEM((4096, 128), BF), pltpu.VMEM((512, 128), BF)],
        compiler_params=pltpu.CompilerParams(vmem_limit_bytes=LIMIT),
        name="prep",
    )(count, rows, w)


def gather_kernel(x, g, ss, zs, ys, ks, ls):
    z, yl, k, col = place()
    up, down = lax.rem(z + 1, 8), lax.rem(z + 7, 8)

    def dev(zz, yy, kk):
        return (zz * 4 + yy * 2 + kk, col)

    along = (dev(up, yl, k), dev(down, yl, k))
    across, sibling = dev(z, 1 - yl, k), dev(z, yl, 1 - k)
    greet((*along, across, sibling))

    def at(zz, yy):
        return pl.multiple_of((zz * 4 + yy * 2 + k) * ND, ND)

    sent = []
    last = {}

    def send(src, base, lo, n, sem, target):
        cp = pltpu.make_async_remote_copy(
            src_ref=x.at[pl.ds(lo, n)] if src is x else g.at[pl.ds(base + lo, n)],
            dst_ref=g.at[pl.ds(base + lo, n)],
            send_sem=ss.at[len(sent)],
            recv_sem=sem,
            device_id=target,
            device_id_type=MESH,
        )
        cp.start()
        sent.append(cp)
        return cp

    to_sibling = []

    def share(src, base, lo, n):
        to_sibling.append(send(src, base, lo, n, ks.at[len(to_sibling)], sibling))

    own = at(z, yl)
    for part in range(2):
        lo = part * 256
        last["y", part] = send(x, own, lo, 256, ys.at[part], across)
        for d in range(2):
            last[d, 1, part] = send(x, own, lo, 256, zs.at[d, 0, part], along[d])
    share(x, own, 0, 512)
    mine = pltpu.make_async_copy(x, g.at[pl.ds(own, ND)], ls)
    mine.start()

    partner = at(z, 1 - yl)
    last["y", 0].wait_recv()
    for d in range(2):
        last[d, 1, 2] = send(g, partner, 0, 256, zs.at[d, 0, 2], along[d])
    share(g, partner, 0, 256)
    crossing = [(last["y", 1], partner)]
    for step in range(1, 5):
        arriving, crossing = crossing, []
        for part in range(3):
            for d in range(2):
                if (d, step, part) not in last:
                    continue
                zz = lax.rem(z + (8 - step if d == 0 else step), 8)
                base = at(zz, yl if part < 2 else 1 - yl)
                lo, n = (0, 256, 0)[part], 256
                if step == 4 and part == 2:
                    lo, n = d * 128, 128
                last[d, step, part].wait_recv()
                sem = zs.at[d, step, part] if step < 4 else None
                if step < 3:
                    last[d, step + 1, part] = send(g, base, lo, n, sem, along[d])
                elif step == 3 and part == d:
                    last[d, 4, part] = send(g, base, lo, n, sem, along[d])
                elif step == 3 and part == 2:
                    last[d, 4, part] = send(g, base, d * 128, 128, sem, along[d])
                if part == 1:
                    cp = send(g, base, 256, 256, ys.at[2 * step + d], across)
                    crossing.append((cp, at(zz, 1 - yl)))
                share(g, base, lo, n)
        for cp, base in arriving:
            cp.wait_recv()
            share(g, base, 256, 256)
    for cp, base in crossing:
        cp.wait_recv()
        share(g, base, 256, 256)
    for cp in to_sibling:
        cp.wait_recv()
    for cp in sent:
        cp.wait_send()
    mine.wait()


def gather_rows(x):
    return pl.pallas_call(
        gather_kernel,
        out_shape=jax.ShapeDtypeStruct((32 * ND, 128), BF),
        in_specs=[ANY],
        out_specs=ANY,
        scratch_shapes=[
            pltpu.SemaphoreType.DMA((80,)),
            pltpu.SemaphoreType.DMA((2, 4, 3)),
            pltpu.SemaphoreType.DMA((10,)),
            pltpu.SemaphoreType.DMA((40,)),
            pltpu.SemaphoreType.DMA,
        ],
        compiler_params=pltpu.CompilerParams(
            collective_id=0, has_side_effects=True, vmem_limit_bytes=LIMIT
        ),
        name="gather_rows",
    )(x)


def two_blocks(a, b):
    zero = jnp.zeros((64, 128), BF)
    return jnp.concatenate(
        [jnp.concatenate([a, zero], 1), jnp.concatenate([zero, b], 1)], 0
    )


def spread_kernel(near, far, cnt, frm, to, blocks, table, out, acc):
    acc[...] = jnp.zeros_like(acc)

    def block(ref, s):
        return pl.ds(pl.multiple_of(ref[s] * 64, 64), 64)

    @pl.loop(0, (cnt[0] + 4 * UNROLL - 1) // (4 * UNROLL))
    def _(i):
        parts = []
        for u in range(UNROLL):
            g = i * UNROLL + u
            for half in range(2):
                first = 4 * g + near * half
                second = first + far
                both = two_blocks(table[block(frm, first), :], table[block(frm, second), :])
                lhs = blocks[g, half * 64 : half * 64 + 64, :]
                prod = jnp.dot(lhs, both, preferred_element_type=F32)
                parts.append((first, prod[:, :128]))
                parts.append((second, prod[:, 128:]))
        for s, value in parts:
            acc[block(to, s), :] += value

    out[...] = acc[...].astype(BF)


def spread(near, far, n, count, frm, to, blocks, table, name):
    return pl.pallas_call(
        functools.partial(spread_kernel, near, far),
        out_shape=jax.ShapeDtypeStruct((n, 128), BF),
        in_specs=[SMEM, SMEM, SMEM, VMEM, VMEM],
        out_specs=VMEM,
        scratch_shapes=[pltpu.VMEM((n, 128), F32)],
        compiler_params=pltpu.CompilerParams(vmem_limit_bytes=LIMIT),
        name=name,
    )(count, frm, to, blocks, table)


def upright(rows, width):
    eye = lax.broadcasted_iota(jnp.int32, (width, 128), 0) == lax.broadcasted_iota(
        jnp.int32, (width, 128), 1
    )
    return jnp.concatenate(
        [
            jnp.sum(jnp.where(eye, rows[i : i + 1, :], 0.0), axis=1, keepdims=True)
            for i in range(rows.shape[0])
        ],
        0,
    )


def node_kernel(
    raw_part, deg, x, ws, wn, mask, cot,
    hidden, group, own_term, gsum,
    rb, rd, nat, sc, gg, rg, ss, s1, s2, s3, s4, ls,
):
    row, col = lax.axis_index("row"), lax.axis_index("col")
    peers = [lax.rem(col + o, 8) for o in range(8)]
    greet([(row, p) for p in peers[1:]])
    sent = []

    def send(src, dst, sem, o):
        cp = pltpu.make_async_remote_copy(
            src_ref=src,
            dst_ref=dst,
            send_sem=ss.at[len(sent)],
            recv_sem=sem,
            device_id=(row, peers[o]),
            device_id_type=MESH,
        )
        cp.start()
        sent.append(cp)
        return cp

    here = pltpu.make_async_copy(raw_part.at[pl.ds(pl.multiple_of(col * ND, ND), ND)], rb.at[0], ls.at[0])
    here.start()
    got = []
    for o in range(1, 8):
        j = peers[o]
        got.append(send(deg.at[pl.ds(pl.multiple_of(j * 8, 8), 8)], rd.at[o], s2.at[o], o))
        got.append(send(raw_part.at[pl.ds(pl.multiple_of(j * ND, ND), ND)], rb.at[o], s1.at[o], o))
    rd[0] = deg[pl.ds(pl.multiple_of(col * 8, 8), 8), :]
    feats = x[...]
    pre_self = jnp.dot(feats, ws[...], preferred_element_type=F32)
    keep = upright(mask[...].astype(F32), 128)
    here.wait()
    for cp in got:
        cp.wait_recv()
    degree = upright(jnp.sum(rd[...], axis=0), 64)
    raw = rb[0].astype(F32)
    for o in range(1, 8):
        raw = raw + rb[o].astype(F32)
    raw = raw.reshape(8, 2, 32, 128)
    for p in range(2):
        nat[pl.ds(p, 256, stride=2), :] = raw[:, p].reshape(256, 128)
    agg = (nat[...] / degree).astype(BF)
    pre = pre_self + jnp.dot(agg, wn[...], preferred_element_type=F32)
    sig = jax.nn.sigmoid(pre)
    dpre = (cot[...].astype(F32) * keep * sig * (1.0 + pre * (1.0 - sig))).astype(BF)
    nt = (((1,), (1,)), ((), ()))
    tn = (((0,), (0,)), ((), ()))
    nat[...] = lax.dot_general(dpre, wn[...], nt, preferred_element_type=F32) / degree
    for p in range(2):
        part = nat[pl.ds(p, 256, stride=2), :].astype(BF).reshape(8, 32, 128)
        for i in range(8):
            sc[i * 64 + p * 32 : i * 64 + p * 32 + 32, :] = part[i]
    mine = pl.ds(pl.multiple_of(col * ND, ND), ND)
    got = [send(sc, group.at[mine], s3.at[o], o) for o in range(1, 8)]
    stay = pltpu.make_async_copy(sc, group.at[mine], ls.at[1])
    stay.start()
    g_self = lax.dot_general(feats, dpre, tn, preferred_element_type=F32)
    g_neigh = lax.dot_general(agg, dpre, tn, preferred_element_type=F32)
    for i, value in enumerate((g_self[:, :128], g_self[:, 128:], g_neigh[:, :128], g_neigh[:, 128:])):
        gg[i * 128 : i * 128 + 128, :] = value
    grads = []
    for o in range(1, 8):
        j = pl.multiple_of(peers[o] * 64, 64)
        grads.append(send(gg.at[pl.ds(j, 64)], rg.at[o], s4.at[o], o))
    hidden[...] = (pre * sig).astype(BF)
    own_term[...] = lax.dot_general(dpre, ws[...], nt, preferred_element_type=F32)
    total = gg[pl.ds(pl.multiple_of(col * 64, 64), 64), :]
    for o in range(1, 8):
        grads[o - 1].wait_recv()
        total = total + rg[o]
    gsum[...] = total
    for cp in got:
        cp.wait_recv()
    stay.wait()
    for cp in sent:
        cp.wait_send()


def node(raw_part, deg, x, ws, wn, mask, cot):
    return pl.pallas_call(
        node_kernel,
        out_shape=[
            jax.ShapeDtypeStruct((ND, 256), BF),
            jax.ShapeDtypeStruct((8 * ND, 128), BF),
            jax.ShapeDtypeStruct((ND, 128), F32),
            jax.ShapeDtypeStruct((64, 128), F32),
        ],
        in_specs=[ANY, VMEM, VMEM, VMEM, VMEM, VMEM, VMEM],
        out_specs=[VMEM, ANY, VMEM, VMEM],
        scratch_shapes=[
            pltpu.VMEM((8, ND, 128), BF),
            pltpu.VMEM((8, 8, 128), F32),
            pltpu.VMEM((ND, 128), F32),
            pltpu.VMEM((ND, 128), BF),
            pltpu.VMEM((ND, 128), F32),
            pltpu.VMEM((8, 64, 128), F32),
            pltpu.SemaphoreType.DMA((28,)),
            pltpu.SemaphoreType.DMA((8,)),
            pltpu.SemaphoreType.DMA((8,)),
            pltpu.SemaphoreType.DMA((8,)),
            pltpu.SemaphoreType.DMA((8,)),
            pltpu.SemaphoreType.DMA((2,)),
        ],
        compiler_params=pltpu.CompilerParams(
            collective_id=1, has_side_effects=True, vmem_limit_bytes=LIMIT
        ),
        name="node",
    )(raw_part, deg, x, ws, wn, mask, cot)


def scatter_kernel(
    t, own_term, gpart,
    out, grad_self, grad_neigh,
    own, sib, ysrc, yb, zsrc, rz, fsrc, fy, gq, gz, gp, gsl, gall,
    ss, zs, ys, ks, ls, q1, q2, q3, q4,
):
    z, yl, k, col = place()

    def dev(zz, yy, kk, cc=None):
        return (zz * 4 + yy * 2 + kk, col if cc is None else cc)

    zat = [lax.rem(z + e, 8) for e in range(8)]
    cat = [lax.rem(col + o, 8) for o in range(8)]
    along = (dev(zat[7], yl, k), dev(zat[1], yl, k))
    across, sibling = dev(z, 1 - yl, k), dev(z, yl, 1 - k)
    quad = (sibling, across, dev(z, 1 - yl, 1 - k))
    greet(
        [*quad]
        + [dev(zat[e], yl, k) for e in range(1, 8)]
        + [dev(z, yl, k, cat[o]) for o in range(1, 8)]
    )
    sent = []

    def send(src, dst, sem, target):
        cp = pltpu.make_async_remote_copy(
            src_ref=src,
            dst_ref=dst,
            send_sem=ss.at[len(sent)],
            recv_sem=sem,
            device_id=target,
            device_id_type=MESH,
        )
        cp.start()
        sent.append(cp)
        return cp

    loads, sibs = {}, {}
    order = (4, 3, 5, 2, 6, 1, 7, 0)
    for e in order:
        for r in (1, 0):
            yy = yl if r == 0 else 1 - yl
            base = (zat[e] * 4 + yy * 2) * ND
            theirs = pl.ds(pl.multiple_of(base + (1 - k) * ND, ND), ND)
            ours = pl.ds(pl.multiple_of(base + k * ND, ND), ND)
            sibs[e, r] = send(t.at[theirs], sib.at[e, r], ks.at[e, r], sibling)
            loads[e, r] = pltpu.make_async_copy(t.at[ours], own.at[e, r], ls.at[e, r])
            loads[e, r].start()
    quads = [send(gpart, gq.at[i], q1.at[i], quad[i]) for i in range(3)]

    ready = set()

    def mine(e, r, lo, n):
        if (e, r) not in ready:
            loads[e, r].wait()
            sibs[e, r].wait_recv()
            ready.add((e, r))
        return own[e, r, lo : lo + n, :].astype(F32) + sib[e, r, lo : lo + n, :].astype(F32)

    ysent = {}

    def cross(e):
        ysrc[e] = mine(e, 1, 256, 256).astype(BF)
        ysent[e] = send(ysrc.at[e], yb.at[e], ys.at[e], across)

    crossed = set()

    def base_value(e, part, lo, n):
        if part == 2:
            return mine(e, 1, lo, n)
        if part == 0:
            return mine(e, 0, lo, n)
        if e not in crossed:
            ysent[e].wait_recv()
            crossed.add(e)
        return mine(e, 0, 256 + lo, n) + yb[e, lo : lo + n, :].astype(F32)

    zsent = {}

    def piece(d, step, part):
        e = (8 - step) % 8 if d == 0 else step
        lo, n = (0, 256) if (step < 4 or part < 2) else (d * 128, 128)
        value = base_value(e, part, lo, n)
        if step < 3 or (step == 3 and part == d):
            zsent[d, step + 1, part].wait_recv()
            value = value + rz[d, step, part * 256 : part * 256 + 256, :].astype(F32)
        elif step == 3 and part == 2:
            zsent[d, 4, 2].wait_recv()
            more = rz[d, 3, 512 + d * 128 : 640 + d * 128, :].astype(F32)
            halves = [value[:128], value[128:]]
            halves[d] = halves[d] + more
            value = jnp.concatenate(halves, 0)
        at = pl.ds(part * 256 + lo, n)
        zsrc[d, step - 1, at, :] = value.astype(BF)
        zsent[d, step, part] = send(
            zsrc.at[d, step - 1, at], rz.at[d, step - 1, at], zs.at[d, step - 1, part], along[d]
        )

    cross(4)
    piece(0, 4, 2)
    piece(1, 4, 2)
    piece(0, 4, 0)
    cross(3)
    cross(5)
    piece(1, 4, 1)
    cross(2)
    cross(6)
    cross(1)
    cross(7)
    cross(0)
    total = gpart[...]
    for i in range(3):
        quads[i].wait_recv()
        total = total + gq[i]
    gz[...] = total
    zred = {}
    for e in range(1, 8):
        src = gz.at[pl.ds(pl.multiple_of(zat[e] * 8, 8), 8)]
        zred[e] = send(src, gp.at[e], q2.at[e], dev(zat[e], yl, k))
    for part in (2, 0, 1):
        for d in range(2):
            piece(d, 3, part)
    here = pl.ds(pl.multiple_of(z * 8, 8), 8)
    gp[0] = gz[here, :]
    for e in range(1, 8):
        zred[e].wait_recv()
    gsl[here, :] = jnp.sum(gp[...], axis=0)
    zall = [send(gsl.at[here], gsl.at[here], q3.at[e], dev(zat[e], yl, k)) for e in range(1, 8)]
    for part in (2, 0, 1):
        for d in range(2):
            piece(d, 2, part)
    for cp in zall:
        cp.wait_recv()
    slot = pl.ds(pl.multiple_of(col * 64, 64), 64)
    gall[slot, :] = gsl[...]
    call = [send(gsl, gall.at[slot], q4.at[o], dev(z, yl, k, cat[o])) for o in range(1, 8)]
    for part in (2, 0, 1):
        for d in range(2):
            piece(d, 1, part)

    def final(part):
        value = base_value(0, part, 0, 256)
        for d in range(2):
            zsent[d, 1, part].wait_recv()
            value = value + rz[d, 0, part * 256 : part * 256 + 256, :].astype(F32)
        return value

    fsrc[...] = final(2).astype(BF)
    last = send(fsrc, fy, ys.at[8], across)
    for cp in call:
        cp.wait_recv()
    grad_self[:, :128] = gall[:128, :]
    grad_self[:, 128:] = gall[128:256, :]
    grad_neigh[:, :128] = gall[256:384, :]
    grad_neigh[:, 128:] = gall[384:, :]
    first = final(0) + own_term[:256, :]
    out[256:, :] = (final(1) + own_term[256:, :]).astype(BF)
    last.wait_recv()
    out[:256, :] = (first + fy[...].astype(F32)).astype(BF)
    for cp in sent:
        cp.wait_send()


def scatter_rows(t, own_term, gpart):
    return pl.pallas_call(
        scatter_kernel,
        out_shape=[
            jax.ShapeDtypeStruct((ND, 128), BF),
            jax.ShapeDtypeStruct((128, 256), F32),
            jax.ShapeDtypeStruct((128, 256), F32),
        ],
        in_specs=[ANY, VMEM, VMEM],
        out_specs=[VMEM, VMEM, VMEM],
        scratch_shapes=[
            pltpu.VMEM((8, 2, ND, 128), BF),
            pltpu.VMEM((8, 2, ND, 128), BF),
            pltpu.VMEM((8, 256, 128), BF),
            pltpu.VMEM((8, 256, 128), BF),
            pltpu.VMEM((2, 4, 768, 128), BF),
            pltpu.VMEM((2, 4, 768, 128), BF),
            pltpu.VMEM((256, 128), BF),
            pltpu.VMEM((256, 128), BF),
            pltpu.VMEM((3, 64, 128), F32),
            pltpu.VMEM((64, 128), F32),
            pltpu.VMEM((8, 8, 128), F32),
            pltpu.VMEM((64, 128), F32),
            pltpu.VMEM((512, 128), F32),
            pltpu.SemaphoreType.DMA((80,)),
            pltpu.SemaphoreType.DMA((2, 4, 3)),
            pltpu.SemaphoreType.DMA((9,)),
            pltpu.SemaphoreType.DMA((8, 2)),
            pltpu.SemaphoreType.DMA((8, 2)),
            pltpu.SemaphoreType.DMA((3,)),
            pltpu.SemaphoreType.DMA((8,)),
            pltpu.SemaphoreType.DMA((8,)),
            pltpu.SemaphoreType.DMA((8,)),
        ],
        compiler_params=pltpu.CompilerParams(
            collective_id=2, has_side_effects=True, vmem_limit_bytes=LIMIT
        ),
        name="scatter_rows",
    )(t, own_term, gpart)


def shards(
    features,
    self_weight,
    neigh_weight,
    block_row,
    block_col,
    block_count,
    edge_weight,
    train_mask,
    out_cotangent,
):
    rows = block_row.reshape(512)
    cols = block_col.reshape(512)
    count = block_count.reshape(1)
    mask = train_mask.reshape(4, 128)
    zf, zt, deg = prep(count, block_row.reshape(1, 512), edge_weight.reshape(512, 4096))
    gathered = gather_rows(features)
    raw_part = spread(1, 2, 8 * ND, count, cols, rows, zf, gathered, "forward")
    hidden, group, own_term, gsum = node(
        raw_part, deg, features, self_weight, neigh_weight, mask, out_cotangent
    )
    through = spread(2, 1, 32 * ND, count, rows, cols, zt, group, "backward")
    grad_input, grad_self, grad_neigh = scatter_rows(through, own_term, gsum)
    return hidden, grad_input, grad_self, grad_neigh


def solution(mesh):
    in_specs = (
        P(("row", "col"), None),
        P(),
        P(),
        P("row", "col", None),
        P("row", "col", None),
        P("row", "col"),
        P("row", "col", None, None),
        P(("row", "col")),
        P(("row", "col"), None),
    )
    out_specs = (P(("row", "col"), None), P(("row", "col"), None), P(), P())
    return jax.shard_map(shards, mesh=mesh, in_specs=in_specs, out_specs=out_specs, check_vma=False)
```

time: 695 us -> 143 us (0.21)
  waiting for transfers between devices: 392 us -> 0 us
  other arithmetic: 149 us -> 0 us
  Pallas kernels: 0 us -> 134 us
  local copies, waits for them, and re-layouts: 76.4 us -> 5.78 us
  matrix products: 36 us -> 0 us
  blocking collectives: 20.4 us -> 0 us
  between operations: 15.3 us -> 1.42 us
    reduce_scatter x2 -> x0, waiting for transfers between devices: 170 us -> none  [the longest x1 120 us: shards(): lax.psum_scatter(transposed.astype(jnp.bfloat16), 'row', scatter_dimensio...]
    pallas_call x0 -> x6, Pallas kernels: none -> 134 us  [the longest x1 44.9 us: node(): pl.pallas_call(node_kernel, out_shape=[jax.ShapeDtypeStruct((ND, 256), BF...]
    scatter-add x3 -> x0, other arithmetic: 133 us -> none  [the longest x1 79.3 us: backward_slots(): jax.ops.segment_sum(contrib, cols_in, num_segments=tile_cols // BLOCK)]
    psum x1 -> x0, waiting for transfers between devices: 131 us -> none  [shards(): lax.psum((grad_self_part, grad_neigh_part), ('row', 'col'))]
    all_gather x2 -> x0, waiting for transfers between devices: 90.4 us -> none  [the longest x1 50.1 us: shards(): scaled_group = lax.all_gather(scaled, 'col', axis=0, tiled=True)]
    gather x2 -> x0, local copies, waits for them, and re-layouts: 43.1 us -> none  [the longest x1 22 us: forward_slots(): blocks = gathered.reshape(-1, BLOCK, width)[cols_in]]
    dot_general x8 -> x0, matrix products: 36 us -> none  [the longest x1 14.4 us: forward_slots(): jnp.einsum('sab,sbd->sad', wmat, blocks, preferred_element_type=jnp.float32)]
    unnamed x1 -> x0, blocking collectives: 20.4 us -> none
  transfers between devices with their start and end apart: 5 -> 0, of which waited for: 5 -> 0; matrix products, arithmetic and copies ran while one was open for 24% -> 0% of each run, Pallas kernels for 0% -> 0%
where the time goes in v1:
time: 143 us; the launch traced here: 141 us
  Pallas kernels  134 us (94%)
  local copies, waits for them, and re-layouts  5.78 us (4%)
    pallas_call x1, Pallas kernels, node(): pl.pallas_call(node_kernel, out_shape=[jax.ShapeDtypeStruct((ND, 256), BF...  44.9 us
    pallas_call x1, Pallas kernels, gather_rows(): pl.pallas_call(gather_kernel, out_shape=jax.ShapeDtypeStruct((32 * ND, 12...  31.8 us
    pallas_call x1, Pallas kernels, scatter_rows(): pl.pallas_call(scatter_kernel, out_shape=[jax.ShapeDtypeStruct((ND, 128),...  28.2 us
    pallas_call x1, Pallas kernels, prep(): pl.pallas_call(prep_kernel, grid=(8,), in_specs=[SMEM, pl.BlockSpec((1, 5...  18.1 us
    pallas_call x2, Pallas kernels, spread(): pl.pallas_call(functools.partial(spread_kernel, near, far), out_shape=jax...  11.1 us
    unnamed x24, local copies, waits for them, and re-layouts  5.78 us

profile of v1, /device:TPU:1, one launch (start us, length us, event | category | flops | bytes accessed | tf_op | source)
XLA Modules:
  0.0 141.3 jit_solution(17721167421535488050)
XLA Ops:
  0.6 0.0 copy-start.7
  1.3 0.0 copy-start.2
  1.3 0.9 copy-done.2
  2.2 31.8 %gather_rows.1.table = bf16[16384,128]{1,0:T(8,128)(2,1)} custom-call(bf16[512,128]{1,0:T(8,128)(2,1)S(1)} %copy-done.2), custom_call_target="tpu_custom_call" | custom-call | tf_op jit(solution)/shard_map/gather_rows/pallas_call | solution.py:187
  34.0 0.0 copy-done.7
  34.0 0.0 copy-start.8
  34.0 18.1 %prep.1 = (bf16[128,128,128]{2,1,0:T(8,128)(2,1)}, bf16[128,128,128]{2,1,0:T(8,128)(2,1)}, f32[64,128]{1,0:T(8,128)S(1)}) custom-call(s32[1]{0:T(128)} %bitcast.6.cnt, s32[1,512]{1,0:T(1,128)S(1)} %bitcast.9, s32[512,4096]{1,0:T(8,128)} %bitcast.15), custom_call_target="tpu_custom_call" | custom-call | tf_op jit(solution)/shard_map/prep/pallas_call | solution.py:78
  52.1 0.0 copy-done.8
  52.2 0.0 copy-start.5
  52.2 0.0 copy-start.6
  52.2 0.0 copy-start.9
  52.2 4.9 %forward.1.raw_part = bf16[4096,128]{1,0:T(8,128)(2,1)S(1)} custom-call(s32[1]{0:T(128)} %bitcast.7.cnt, s32[512]{0:T(512)S(1)} %bitcast.12, s32[512]{0:T(512)S(1)} %bitcast.10, bf16[128,128,128]{2,1,0:T(8,128)(2,1)} %get-tuple-element.14.blocks, bf16[16384,128]{1,0:T(8,128)(2,1)} %gather_rows.1.table), custom_call_target="tpu_custom_call" | custom-call | tf_op jit(solution)/shard_map/forward/pallas_call | solution.py:239
  57.1 0.0 copy-start
  57.1 1.0 copy-done
  58.0 0.0 copy-done.6
  58.0 0.0 copy-done.9
  58.1 44.9 %node.1 = (bf16[512,256]{1,0:T(8,128)(2,1)S(1)}, bf16[4096,128]{1,0:T(8,128)(2,1)}, f32[512,128]{1,0:T(8,128)S(1)}, f32[64,128]{1,0:T(8,128)S(1)}) custom-call(bf16[4096,128]{1,0:T(8,128)(2,1)} %copy-done, f32[64,128]{1,0:T(8,128)S(1)} %get-tuple-element.15.deg, bf16[512,128]{1,0:T(8,128)(2,1)S(1)} %copy-done.3, bf16[128,256]{1,0:T(8,128)(2,1)S(1)} %copy-done.5, ...), custom_call_target="tpu_custom_call" | custom-call | tf_op jit(solution)/shard_map/node/pallas_call | solution.py:345
  103.0 1.2 copy-done.1
  104.2 6.2 %backward.1.t = bf16[16384,128]{1,0:T(8,128)(2,1)} custom-call(s32[1]{0:T(128)} %bitcast.8.cnt, s32[512]{0:T(512)S(1)} %bitcast.11, s32[512]{0:T(512)S(1)} %bitcast.13, bf16[128,128,128]{2,1,0:T(8,128)(2,1)} %get-tuple-element.17.blocks, bf16[4096,128]{1,0:T(8,128)(2,1)S(1)} %copy-done.1), custom_call_target="tpu_custom_call" | custom-call | tf_op jit(solution)/shard_map/backward/pallas_call | solution.py:239
  110.4 28.2 %scatter_rows.1 = (bf16[512,128]{1,0:T(8,128)(2,1)S(1)}, f32[128,256]{1,0:T(8,128)S(1)}, f32[128,256]{1,0:T(8,128)S(1)}) custom-call(bf16[16384,128]{1,0:T(8,128)(2,1)} %backward.1.t, f32[512,128]{1,0:T(8,128)S(1)} %get-tuple-element.19.own_term, f32[64,128]{1,0:T(8,128)S(1)} %get-tuple-element.20.gpart), custom_call_target="tpu_custom_call" | custom-call | tf_op jit(solution)/shard_map/scatter_rows/pallas_call | solution.py:539
  138.7 0.7 copy.18
  139.4 0.7 copy.19
  140.0 0.7 copy.20
  140.7 0.7 copy.21
  (6 shorter events, 0.0 us)
Async XLA Ops:
  0.6 33.4 %copy-start.7 = (s32[1,1,512]{2,1,0:T(1,128)S(1)}, s32[1,1,512]{2,1,0:T(1,128)}, u32[]{:S(2)}) copy-start(s32[1,1,512]{2,1,0:T(1,128)} %param.12) | copy-start | bytes 6148
  1.3 0.9 copy-start.2
  34.0 18.1 %copy-start.8 = (s32[1,1,512]{2,1,0:T(1,128)S(1)}, s32[1,1,512]{2,1,0:T(1,128)}, u32[]{:S(2)}) copy-start(s32[1,1,512]{2,1,0:T(1,128)} %param.13) | copy-start | bytes 6148
  52.1 5.9 %copy-start.3 = (bf16[512,128]{1,0:T(8,128)(2,1)S(1)}, bf16[512,128]{1,0:T(8,128)(2,1)}, u32[]{:S(2)}) copy-start(bf16[512,128]{1,0:T(8,128)(2,1)} %x.3) | copy-start | bytes 393220
  52.1 5.9 %copy-start.4 = (bf16[512,256]{1,0:T(8,128)(2,1)S(1)}, bf16[512,256]{1,0:T(8,128)(2,1)}, u32[]{:S(2)}) copy-start(bf16[512,256]{1,0:T(8,128)(2,1)} %cot.1) | copy-start | bytes 786436
  52.2 5.9 %copy-start.5 = (bf16[128,256]{1,0:T(8,128)(2,1)S(1)}, bf16[128,256]{1,0:T(8,128)(2,1)}, u32[]{:S(2)}) copy-start(bf16[128,256]{1,0:T(8,128)(2,1)} %ws.1) | copy-start | bytes 196612
  52.2 5.9 %copy-start.6 = (bf16[128,256]{1,0:T(8,128)(2,1)S(1)}, bf16[128,256]{1,0:T(8,128)(2,1)}, u32[]{:S(2)}) copy-start(bf16[128,256]{1,0:T(8,128)(2,1)} %wn.1) | copy-start | bytes 196612
  52.2 5.9 %copy-start.9 = (s32[512]{0:T(512)S(1)}, s32[512]{0:T(512)}, u32[]{:S(2)}) copy-start(s32[512]{0:T(512)} %param.16) | copy-start | bytes 6148
  57.1 1.0 copy-start
  103.0 1.2 copy-start.1

commit v2 on v1

v2 whole, which is shorter than its diff:
```python
import functools

import jax
import jax.numpy as jnp
from jax import lax
from jax.experimental import pallas as pl
from jax.experimental.pallas import tpu as pltpu
from jax.sharding import PartitionSpec as P

MESH = pl.DeviceIdType.MESH
BF = jnp.bfloat16
F32 = jnp.float32
VMEM = pl.BlockSpec(memory_space=pltpu.VMEM)
SMEM = pl.BlockSpec(memory_space=pltpu.SMEM)
ANY = pl.BlockSpec(memory_space=pl.ANY)
ND = 512
UNROLL = 16
WORK = (8, 3, 3, 2, 2)
TURN = (32, 32, 24)


def place():
    row = lax.axis_index("row")
    return row // 4, (row // 2) % 2, row % 2, lax.axis_index("col")


def greet(targets):
    barrier = pltpu.get_barrier_semaphore()
    for target in targets:
        pl.semaphore_signal(barrier, inc=1, device_id=target, device_id_type=MESH)
    pl.semaphore_wait(barrier, len(targets))


def sender(ss):
    sent = []

    def send(src, dst, sem, target):
        cp = pltpu.make_async_remote_copy(
            src_ref=src,
            dst_ref=dst,
            send_sem=ss.at[len(sent)],
            recv_sem=sem,
            device_id=target,
            device_id_type=MESH,
        )
        cp.start()
        sent.append(cp)
        return cp

    return send, sent


def ring_gather(half, x, table, base, send, zs, ys, along, across, share, idle):
    last = {}

    def go(src, row, lo, n, sem, target):
        return send(
            x.at[pl.ds(lo, n)] if src is x else table.at[pl.ds(row + lo, n)],
            table.at[pl.ds(row + lo, n)],
            sem,
            target,
        )

    own, partner = base(0, 0), base(0, 1)
    first = go(x, own, 0, 256, ys.at[0], across)
    for part in (1, 0):
        for d in range(2):
            last[d, 1, part] = go(x, own, part * 256, 256, zs.at[d, 0, part], along[d])
    crossing = [(go(x, own, 256, 256, ys.at[1], across), partner)]
    share(x, own, 0, 512)
    idle(0)
    first.wait_recv()
    for d in range(2):
        last[d, 1, 2] = go(table, partner, 0, 256, zs.at[d, 0, 2], along[d])
    share(table, partner, 0, 256)
    for step in range(1, half + 1):
        arriving, crossing = crossing, []
        for part in (1, 2, 0):
            for d in range(2):
                if (d, step, part) not in last:
                    continue
                e = 2 * half - step if d == 0 else step
                row = base(e, 0 if part < 2 else 1)
                lo, n = (0, 256, 0)[part], 256
                if step == half and part == 2:
                    lo, n = d * 128, 128
                last[d, step, part].wait_recv()
                if step < half - 1 or (step == half - 1 and part == d):
                    last[d, step + 1, part] = go(table, row, lo, n, zs.at[d, step, part], along[d])
                elif step == half - 1 and part == 2:
                    last[d, half, 2] = go(table, row, d * 128, 128, zs.at[d, step, 2], along[d])
                if part == 1:
                    cp = go(table, row, 256, 256, ys.at[2 * step + d], across)
                    crossing.append((cp, base(e, 1)))
                share(table, row, lo, n)
                idle(step)
        for cp, row in arriving:
            cp.wait_recv()
            share(table, row, 256, 256)
    for cp, row in crossing:
        cp.wait_recv()
        share(table, row, 256, 256)


def ring_reduce(half, value, direct, zsrc, rz, send, zs, along):
    zsent = {}

    def arrived(d, step, part, lo, n):
        return rz[d, step, part * 256 + lo : part * 256 + lo + n, :].astype(F32)

    def piece(d, step, part):
        e = (2 * half - step) if d == 0 else step
        lo, n = (0, 256) if (step < half or part < 2) else (d * 128, 128)
        at = pl.ds(part * 256 + lo, n)
        alone = step == half or (step == half - 1 and part == 1 - d)
        src = direct(e, part, lo, n) if alone else None
        if src is None:
            total = value(e, part, lo, n)
            if step < half - 1 or (step == half - 1 and part == d):
                zsent[d, step + 1, part].wait_recv()
                total = total + arrived(d, step, part, 0, 256)
            elif step == half - 1 and part == 2:
                zsent[d, half, 2].wait_recv()
                halves = [total[:128], total[128:]]
                halves[d] = halves[d] + arrived(d, step, 2, d * 128, 128)
                total = jnp.concatenate(halves, 0)
            zsrc[d, step - 1, at, :] = total.astype(BF)
            src = zsrc.at[d, step - 1, at]
        zsent[d, step, part] = send(src, rz.at[d, step - 1, at], zs.at[d, step - 1, part], along[d])

    def final(part):
        total = value(0, part, 0, 256)
        for d in range(2):
            zsent[d, 1, part].wait_recv()
            total = total + arrived(d, 0, part, 0, 256)
        return total

    return piece, final


def gather_kernel(
    cnt, rows, x, w,
    g, zf, deg,
    wv, pat, dsl, ss, zs, ys, ks, ls, wsem,
):
    z, yl, k, col = place()

    def dev(zz, yy, kk):
        return (zz * 4 + yy * 2 + kk, col)

    slabs = []
    for i in range(8):
        slabs.append(pltpu.make_async_copy(w.at[pl.ds(i * 64, 64)], wv.at[pl.ds(i * 64, 64)], wsem.at[i]))
        slabs[-1].start()
    along = (dev(lax.rem(z + 1, 8), yl, k), dev(lax.rem(z + 7, 8), yl, k))
    across, sibling = dev(z, 1 - yl, k), dev(z, yl, 1 - k)
    greet((*along, across, sibling))
    send, sent = sender(ss)

    def base(e, r):
        yy = yl if r == 0 else 1 - yl
        return pl.multiple_of((lax.rem(z + e, 8) * 4 + yy * 2 + k) * ND, ND)

    to_sibling = []

    def share(src, row, lo, n):
        at = pl.ds(row + lo, n)
        src = x.at[pl.ds(lo, n)] if src is x else g.at[at]
        to_sibling.append(send(src, g.at[at], ks.at[len(to_sibling)], sibling))

    low = lax.broadcasted_iota(jnp.int32, (32, 128), 1) < 64
    lim = cnt[0]
    done = [0]

    def unit(i):
        b = pl.multiple_of(i * 8, 8)
        live = (b + lax.broadcasted_iota(jnp.int32, (8, 4096), 0)) < lim
        y = jnp.where(live, wv[pl.ds(b, 8), :], 0).astype(F32).reshape(8, 32, 128)
        for h4 in range(2):
            y4 = [y[h4 * 4 + s] for s in range(4)]
            r4 = [pltpu.roll(v, 64, 1) for v in y4]
            zf[i * 2 + h4] = jnp.concatenate(
                [
                    jnp.where(low, y4[0], r4[2]),
                    jnp.where(low, r4[0], y4[2]),
                    jnp.where(low, y4[1], r4[3]),
                    jnp.where(low, r4[1], y4[3]),
                ],
                0,
            ).astype(BF)

    def work(n):
        n = min(n, 64 - done[0])
        if n <= 0:
            return
        lo = done[0]
        for i in range(lo // 8 if lo % 8 == 0 else lo // 8 + 1, (lo + n - 1) // 8 + 1):
            slabs[i].wait()
        pl.loop(lo, lo + n)(unit)
        for i in range(lo // 8, (lo + n) // 8):
            at = pl.ds(i * 64, 64)
            dsl[at, :] = jnp.dot(
                wv[at, :].astype(F32).astype(BF), pat[...], preferred_element_type=F32
            ).astype(BF)
        done[0] += n

    def idle(step):
        work(WORK[step])

    def prepare(step):
        if step == 0:
            at = lax.broadcasted_iota(jnp.int32, (4096, 128), 0) // 64
            pat[...] = (at == lax.broadcasted_iota(jnp.int32, (4096, 128), 1)).astype(BF)
        idle(step)

    mine = pltpu.make_async_copy(x, g.at[pl.ds(base(0, 0), ND)], ls)
    mine.start()
    ring_gather(4, x, g, base, send, zs, ys, along, across, share, prepare)
    work(64)
    slot = lax.broadcasted_iota(jnp.int32, (64, 512), 1)
    hot = (lax.broadcasted_iota(jnp.int32, (64, 512), 0) == rows[...]) & (slot < lim)
    deg[...] = jnp.dot(hot.astype(F32).astype(BF), dsl[...], preferred_element_type=F32)
    for cp in to_sibling:
        cp.wait_recv()
    for cp in sent:
        cp.wait_send()
    mine.wait()


def gather_rows(count, rows, x, w):
    return pl.pallas_call(
        gather_kernel,
        out_shape=[
            jax.ShapeDtypeStruct((32 * ND, 128), BF),
            jax.ShapeDtypeStruct((128, 128, 128), BF),
            jax.ShapeDtypeStruct((64, 128), F32),
        ],
        in_specs=[SMEM, VMEM, ANY, pl.BlockSpec(memory_space=pltpu.HBM)],
        out_specs=[ANY, VMEM, VMEM],
        scratch_shapes=[
            pltpu.VMEM((512, 4096), jnp.int32),
            pltpu.VMEM((4096, 128), BF),
            pltpu.VMEM((512, 128), BF),
            pltpu.SemaphoreType.DMA((80,)),
            pltpu.SemaphoreType.DMA((2, 4, 3)),
            pltpu.SemaphoreType.DMA((10,)),
            pltpu.SemaphoreType.DMA((40,)),
            pltpu.SemaphoreType.DMA,
            pltpu.SemaphoreType.DMA((8,)),
        ],
        compiler_params=pltpu.CompilerParams(
            collective_id=0, has_side_effects=True, vmem_limit_bytes=43 << 20
        ),
        name="gather_rows",
    )(count, rows, x, w)


def two_blocks(a, b):
    zero = jnp.zeros((64, 128), BF)
    return jnp.concatenate(
        [jnp.concatenate([a, zero], 1), jnp.concatenate([zero, b], 1)], 0
    )


def spread_kernel(near, far, cnt, frm, to, blocks, table, out, acc):
    acc[...] = jnp.zeros_like(acc)

    def block(ref, s):
        return pl.ds(pl.multiple_of(ref[s] * 64, 64), 64)

    @pl.loop(0, (cnt[0] + 4 * UNROLL - 1) // (4 * UNROLL))
    def _(i):
        parts = []
        for u in range(UNROLL):
            g = i * UNROLL + u
            for half in range(2):
                first = 4 * g + near * half
                second = first + far
                both = two_blocks(table[block(frm, first), :], table[block(frm, second), :])
                lhs = blocks[g, half * 64 : half * 64 + 64, :]
                prod = jnp.dot(lhs, both, preferred_element_type=F32)
                parts.append((first, prod[:, :128]))
                parts.append((second, prod[:, 128:]))
        for s, value in parts:
            acc[block(to, s), :] += value

    out[...] = acc[...].astype(BF)


def forward(count, frm, to, blocks, table):
    return pl.pallas_call(
        functools.partial(spread_kernel, 1, 2),
        out_shape=jax.ShapeDtypeStruct((8 * ND, 128), BF),
        in_specs=[SMEM, SMEM, SMEM, VMEM, VMEM],
        out_specs=VMEM,
        scratch_shapes=[pltpu.VMEM((8 * ND, 128), F32)],
        compiler_params=pltpu.CompilerParams(vmem_limit_bytes=16 << 20),
        name="forward",
    )(count, frm, to, blocks, table)


def backward_kernel(cnt, frm, to, blocks, table, hidden, out, kept, acc, sem):
    keep = pltpu.make_async_copy(hidden, kept, sem)
    keep.start()
    spread_kernel(2, 1, cnt, frm, to, blocks, table, out, acc)
    keep.wait()


def backward(count, frm, to, blocks, table, hidden):
    return pl.pallas_call(
        backward_kernel,
        out_shape=[
            jax.ShapeDtypeStruct((32 * ND, 128), BF),
            jax.ShapeDtypeStruct(hidden.shape, hidden.dtype),
        ],
        in_specs=[SMEM, SMEM, SMEM, VMEM, VMEM, ANY],
        out_specs=[VMEM, ANY],
        scratch_shapes=[pltpu.VMEM((32 * ND, 128), F32), pltpu.SemaphoreType.DMA],
        compiler_params=pltpu.CompilerParams(vmem_limit_bytes=20 << 20),
        name="backward",
    )(count, frm, to, blocks, table, hidden)


def upright(rows, width):
    eye = lax.broadcasted_iota(jnp.int32, (width, 128), 0) == lax.broadcasted_iota(
        jnp.int32, (width, 128), 1
    )
    return jnp.concatenate(
        [
            jnp.sum(jnp.where(eye, rows[i : i + 1, :], 0.0), axis=1, keepdims=True)
            for i in range(rows.shape[0])
        ],
        0,
    )


def node_kernel(
    raw_part, deg, x, ws, wn, mask, cot, zf,
    hidden, group, own_term, gsum, zt,
    yb, zsrc, rz, fsrc, fy, rd, nat, sc, grads, gr, ss, z1, y1, z2, y2, ds, gsem, ls,
):
    row, col = lax.axis_index("row"), lax.axis_index("col")
    yh, xx = col // 4, lax.rem(col, 4)
    z, side = row // 4, lax.rem(row, 4)
    zat = [lax.rem(z + e, 8) for e in range(8)]
    xat = [lax.rem(xx + e, 4) for e in range(4)]
    peers = [lax.rem(col + o, 8) for o in range(8)]
    up, down = (row, yh * 4 + xat[1]), (row, yh * 4 + xat[3])
    across = (row, (1 - yh) * 4 + xx)
    greet([(row, p) for p in peers[1:]] + [(zat[e] * 4 + side, col) for e in range(1, 8)])
    send, sent = sender(ss)

    def base(e, r):
        return pl.multiple_of(((yh if r == 0 else 1 - yh) * 4 + xat[e]) * ND, ND)

    def part_ref(e, part, lo, n):
        row0 = base(e, 1 if part == 2 else 0) + (256 if part == 1 else 0)
        return raw_part.at[pl.ds(row0 + lo, n)]

    ysent = {}

    def cross(e):
        ysent[e] = send(raw_part.at[pl.ds(base(e, 1) + 256, 256)], yb.at[e], y1.at[e], across)

    crossed = set()

    def value(e, part, lo, n):
        total = part_ref(e, part, lo, n)[...].astype(F32)
        if part == 1:
            if e not in crossed:
                ysent[e].wait_recv()
                crossed.add(e)
            total = total + yb[e, lo : lo + n, :].astype(F32)
        return total

    def direct(e, part, lo, n):
        return None if part == 1 else part_ref(e, part, lo, n)

    piece, final = ring_reduce(2, value, direct, zsrc, rz, send, z1, (down, up))

    def turn(lo, n):
        @pl.loop(lo, lo + n)
        def _(i):
            zt[i] = zf[i].T

    cross(2)
    piece(0, 2, 2)
    piece(1, 2, 2)
    piece(0, 2, 0)
    cross(1)
    cross(3)
    piece(1, 1, 0)
    cross(0)
    rd[0] = deg[pl.ds(pl.multiple_of(col * 8, 8), 8), :]
    degs = []
    for o in range(1, 8):
        src = deg.at[pl.ds(pl.multiple_of(peers[o] * 8, 8), 8)]
        degs.append(send(src, rd.at[o], ds.at[o], (row, peers[o])))
    feats = x[...]
    pre_self = jnp.dot(feats, ws[...], preferred_element_type=F32)
    keep = upright(mask[...].astype(F32), 128)
    turn(0, TURN[0])
    piece(1, 2, 1)
    piece(0, 1, 1)
    piece(0, 1, 2)
    piece(1, 1, 2)
    piece(0, 1, 0)
    piece(1, 1, 1)
    for cp in degs:
        cp.wait_recv()
    degree = upright(jnp.sum(rd[...], axis=0), 64)
    turn(TURN[0], TURN[1])
    fsrc[...] = final(2).astype(BF)
    last = send(fsrc, fy, y1.at[4], across)
    second = final(1)
    first = final(0)
    turn(TURN[0] + TURN[1], TURN[2])
    last.wait_recv()
    raw = jnp.concatenate([first + fy[...].astype(F32), second], 0).reshape(8, 2, 32, 128)
    for p in range(2):
        nat[pl.ds(p, 256, stride=2), :] = raw[:, p].reshape(256, 128)
    agg = (nat[...] / degree).astype(BF)
    pre = pre_self + jnp.dot(agg, wn[...], preferred_element_type=F32)
    sig = jax.nn.sigmoid(pre)
    dpre = (cot[...].astype(F32) * keep * sig * (1.0 + pre * (1.0 - sig))).astype(BF)
    nt = (((1,), (1,)), ((), ()))
    tn = (((0,), (0,)), ((), ()))
    nat[...] = lax.dot_general(dpre, wn[...], nt, preferred_element_type=F32) / degree
    for p in range(2):
        part = nat[pl.ds(p, 256, stride=2), :].astype(BF).reshape(8, 32, 128)
        for i in range(8):
            sc[i * 64 + p * 32 : i * 64 + p * 32 + 32, :] = part[i]
    stay = pltpu.make_async_copy(sc, group.at[pl.ds(base(0, 0), ND)], ls)
    stay.start()
    todo = []
    slices = []

    def later():
        hidden[...] = (pre * sig).astype(BF)
        own_term[...] = lax.dot_general(dpre, ws[...], nt, preferred_element_type=F32)
        g_self = lax.dot_general(feats, dpre, tn, preferred_element_type=F32)
        g_neigh = lax.dot_general(agg, dpre, tn, preferred_element_type=F32)
        for i, v in enumerate((g_self[:, :128], g_self[:, 128:], g_neigh[:, :128], g_neigh[:, 128:])):
            grads[i * 128 : i * 128 + 128, :] = v
        for e in range(1, 8):
            src = grads.at[pl.ds(pl.multiple_of(zat[e] * 64, 64), 64)]
            slices.append(send(src, gr.at[e], gsem.at[e], (zat[e] * 4 + side, col)))

    def idle(step):
        if step == 0:
            later()
        elif not todo:
            todo.append(1)
            turn(sum(TURN[:3]), 128 - sum(TURN[:3]))

    ring_gather(
        2, sc, group, base, send, z2, y2, (up, down), across, lambda *a: None, idle
    )
    total = grads[pl.ds(pl.multiple_of(z * 64, 64), 64), :]
    for e in range(1, 8):
        slices[e - 1].wait_recv()
        total = total + gr[e]
    gsum[...] = total
    stay.wait()
    for cp in sent:
        cp.wait_send()


def node(raw_part, deg, x, ws, wn, mask, cot, zf):
    return pl.pallas_call(
        node_kernel,
        out_shape=[
            jax.ShapeDtypeStruct((ND, 256), BF),
            jax.ShapeDtypeStruct((8 * ND, 128), BF),
            jax.ShapeDtypeStruct((ND, 128), F32),
            jax.ShapeDtypeStruct((64, 128), F32),
            jax.ShapeDtypeStruct((128, 128, 128), BF),
        ],
        in_specs=[VMEM] * 8,
        out_specs=[VMEM, ANY, VMEM, VMEM, VMEM],
        scratch_shapes=[
            pltpu.VMEM((4, 256, 128), BF),
            pltpu.VMEM((2, 2, 768, 128), BF),
            pltpu.VMEM((2, 2, 768, 128), BF),
            pltpu.VMEM((256, 128), BF),
            pltpu.VMEM((256, 128), BF),
            pltpu.VMEM((8, 8, 128), F32),
            pltpu.VMEM((ND, 128), F32),
            pltpu.VMEM((ND, 128), BF),
            pltpu.VMEM((512, 128), F32),
            pltpu.VMEM((8, 64, 128), F32),
            pltpu.SemaphoreType.DMA((60,)),
            pltpu.SemaphoreType.DMA((2, 2, 3)),
            pltpu.SemaphoreType.DMA((5,)),
            pltpu.SemaphoreType.DMA((2, 2, 3)),
            pltpu.SemaphoreType.DMA((6,)),
            pltpu.SemaphoreType.DMA((8,)),
            pltpu.SemaphoreType.DMA((8,)),
            pltpu.SemaphoreType.DMA,
        ],
        compiler_params=pltpu.CompilerParams(
            collective_id=1, has_side_effects=True, vmem_limit_bytes=20 << 20
        ),
        name="node",
    )(raw_part, deg, x, ws, wn, mask, cot, zf)


def in_order(parts, me, n):
    total = None
    for p in range(n):
        i = lax.rem(me - p - 1 + 2 * n, n)
        total = parts[i] if total is None else total + parts[i]
    return total


def scatter_kernel(
    t, own_term, gpart,
    out, grad_self, grad_neigh,
    own, sib, ysrc, yb, zsrc, rz, fsrc, fy, gk, gx, gy, gsrc, gall,
    ss, zs, ys, ks, ls, q0, q1, q2, q3,
):
    z, yl, k, col = place()

    def dev(zz, yy, kk, cc=None):
        return (zz * 4 + yy * 2 + kk, col if cc is None else cc)

    zat = [lax.rem(z + e, 8) for e in range(8)]
    yh, xx = col // 4, lax.rem(col, 4)
    along = (dev(zat[7], yl, k), dev(zat[1], yl, k))
    across, sibling = dev(z, 1 - yl, k), dev(z, yl, 1 - k)
    far = (1 - yh) * 4 + xx
    ypeers = (across, dev(z, yl, k, far), dev(z, 1 - yl, k, far))
    xpeers = [dev(z, yl, k, yh * 4 + lax.rem(xx + e, 4)) for e in (1, 2, 3)]
    zpeers = [dev(zat[e], yl, k) for e in range(1, 8)]
    greet([sibling, *ypeers, *xpeers, *zpeers])
    send, sent = sender(ss)
    theirs = pl.ds(pl.multiple_of((1 - k) * 32, 32), 32)
    ours = pl.ds(pl.multiple_of(k * 32, 32), 32)
    halves = send(gpart.at[theirs], gk, q0.at[0], sibling)

    loads, sibs = {}, {}
    for e in (4, 3, 5, 2, 6, 1, 7, 0):
        for r in (1, 0):
            yy = yl if r == 0 else 1 - yl
            row = (zat[e] * 4 + yy * 2) * ND
            theirs = pl.ds(pl.multiple_of(row + (1 - k) * ND, ND), ND)
            ours = pl.ds(pl.multiple_of(row + k * ND, ND), ND)
            sibs[e, r] = send(t.at[theirs], sib.at[e, r], ks.at[e, r], sibling)
            loads[e, r] = pltpu.make_async_copy(t.at[ours], own.at[e, r], ls.at[e, r])
            loads[e, r].start()
    ready = set()

    def mine(e, r, lo, n):
        if (e, r) not in ready:
            loads[e, r].wait()
            sibs[e, r].wait_recv()
            ready.add((e, r))
        return own[e, r, lo : lo + n, :].astype(F32) + sib[e, r, lo : lo + n, :].astype(F32)

    ysent = {}

    def cross(e):
        ysrc[e] = mine(e, 1, 256, 256).astype(BF)
        ysent[e] = send(ysrc.at[e], yb.at[e], ys.at[e], across)

    crossed = set()

    def value(e, part, lo, n):
        if part == 2:
            return mine(e, 1, lo, n)
        if part == 0:
            return mine(e, 0, lo, n)
        if e not in crossed:
            ysent[e].wait_recv()
            crossed.add(e)
        return mine(e, 0, 256 + lo, n) + yb[e, lo : lo + n, :].astype(F32)

    piece, final = ring_reduce(4, value, lambda *a: None, zsrc, rz, send, zs, along)

    cross(4)
    piece(0, 4, 2)
    piece(1, 4, 2)
    piece(0, 4, 0)
    cross(3)
    cross(5)
    piece(1, 4, 1)
    cross(2)
    cross(6)
    cross(1)
    cross(7)
    cross(0)
    halves.wait_recv()
    total = gpart[pl.ds(pl.multiple_of(k * 32, 32), 32), :] + gk[...]
    gsrc[0] = total
    swaps = [send(gsrc.at[0], gx.at[i], q1.at[i], xpeers[i]) for i in range(3)]
    for part in (2, 0, 1):
        for d in range(2):
            piece(d, 3, part)
    gx[3] = gsrc[0]
    for cp in swaps:
        cp.wait_recv()
    total = in_order(gx, xx, 4)
    gsrc[1] = total
    swaps = [send(gsrc.at[1], gy.at[i], q2.at[i], ypeers[i]) for i in range(3)]
    for part in (2, 0, 1):
        for d in range(2):
            piece(d, 2, part)
    for cp in swaps:
        cp.wait_recv()
    total = (gsrc[1] + gy[0]) + (gy[1] + gy[2])
    mine_at = gall.at[z, k]
    gall[z, k] = total
    swaps = [send(mine_at, mine_at, q3.at[i], zpeers[i]) for i in range(7)]
    for part in (2, 0, 1):
        for d in range(2):
            piece(d, 1, part)
    fsrc[...] = final(2).astype(BF)
    last = send(fsrc, fy, ys.at[8], across)
    first = final(0) + own_term[:256, :]
    out[256:, :] = (final(1) + own_term[256:, :]).astype(BF)
    for cp in swaps:
        cp.wait_recv()
    other = send(gall.at[:, k], gall.at[:, k], q0.at[1], sibling)
    last.wait_recv()
    out[:256, :] = (first + fy[...].astype(F32)).astype(BF)
    other.wait_recv()
    for i, ref in enumerate((grad_self, grad_neigh)):
        for h in range(2):
            lo = i * 4 + h * 2
            ref[:, h * 128 : h * 128 + 128] = gall[lo : lo + 2].reshape(128, 128)
    for cp in sent:
        cp.wait_send()


def scatter_rows(t, own_term, grads):
    return pl.pallas_call(
        scatter_kernel,
        out_shape=[
            jax.ShapeDtypeStruct((ND, 128), BF),
            jax.ShapeDtypeStruct((128, 256), F32),
            jax.ShapeDtypeStruct((128, 256), F32),
        ],
        in_specs=[ANY, VMEM, VMEM],
        out_specs=[VMEM, VMEM, VMEM],
        scratch_shapes=[
            pltpu.VMEM((8, 2, ND, 128), BF),
            pltpu.VMEM((8, 2, ND, 128), BF),
            pltpu.VMEM((8, 256, 128), BF),
            pltpu.VMEM((8, 256, 128), BF),
            pltpu.VMEM((2, 4, 768, 128), BF),
            pltpu.VMEM((2, 4, 768, 128), BF),
            pltpu.VMEM((256, 128), BF),
            pltpu.VMEM((256, 128), BF),
            pltpu.VMEM((32, 128), F32),
            pltpu.VMEM((4, 32, 128), F32),
            pltpu.VMEM((3, 32, 128), F32),
            pltpu.VMEM((2, 32, 128), F32),
            pltpu.VMEM((8, 2, 32, 128), F32),
            pltpu.SemaphoreType.DMA((90,)),
            pltpu.SemaphoreType.DMA((2, 4, 3)),
            pltpu.SemaphoreType.DMA((9,)),
            pltpu.SemaphoreType.DMA((8, 2)),
            pltpu.SemaphoreType.DMA((8, 2)),
            pltpu.SemaphoreType.DMA((2,)),
            pltpu.SemaphoreType.DMA((3,)),
            pltpu.SemaphoreType.DMA((3,)),
            pltpu.SemaphoreType.DMA((7,)),
        ],
        compiler_params=pltpu.CompilerParams(
            collective_id=2, has_side_effects=True, vmem_limit_bytes=20 << 20
        ),
        name="scatter_rows",
    )(t, own_term, grads)


def finish_kernel(*refs):
    n = len(refs) // 2
    sem = refs[-1]
    copies = [pltpu.make_async_copy(refs[i], refs[n + i], sem.at[i]) for i in range(n)]
    for cp in copies:
        cp.start()
    for cp in copies:
        cp.wait()


def finish(*arrays):
    return pl.pallas_call(
        finish_kernel,
        out_shape=[jax.ShapeDtypeStruct(a.shape, a.dtype) for a in arrays],
        in_specs=[VMEM] * len(arrays),
        out_specs=[ANY] * len(arrays),
        scratch_shapes=[pltpu.SemaphoreType.DMA((len(arrays),))],
        compiler_params=pltpu.CompilerParams(vmem_limit_bytes=16 << 20),
        name="finish",
    )(*arrays)


def shards(
    features,
    self_weight,
    neigh_weight,
    block_row,
    block_col,
    block_count,
    edge_weight,
    train_mask,
    out_cotangent,
):
    rows = block_row.reshape(512)
    cols = block_col.reshape(512)
    count = block_count.reshape(1)
    mask = train_mask.reshape(4, 128)
    gathered, zf, deg = gather_rows(
        count, block_row.reshape(1, 512), features, edge_weight.reshape(512, 4096)
    )
    raw_part = forward(count, cols, rows, zf, gathered)
    hidden, group, own_term, grads, zt = node(
        raw_part, deg, features, self_weight, neigh_weight, mask, out_cotangent, zf
    )
    through, hidden = backward(count, rows, cols, zt, group, hidden)
    return hidden, *finish(*scatter_rows(through, own_term, grads))


def solution(mesh):
    in_specs = (
        P(("row", "col"), None),
        P(),
        P(),
        P("row", "col", None),
        P("row", "col", None),
        P("row", "col"),
        P("row", "col", None, None),
        P(("row", "col")),
        P(("row", "col"), None),
    )
    out_specs = (P(("row", "col"), None), P(("row", "col"), None), P(), P())
    return jax.shard_map(shards, mesh=mesh, in_specs=in_specs, out_specs=out_specs, check_vma=False)
```

time: 143 us -> 113 us (0.79); the launches traced: 141 us -> 113 us
  Pallas kernels: 134 us -> 110 us
  local copies, waits for them, and re-layouts: 5.78 us -> 1.61 us
    pallas_call x4, Pallas kernels: 61 us -> 43.2 us  [the longest x1 31 us: gather_rows(): pl.pallas_call(gather_kernel, out_shape=[jax.ShapeDtypeStruct((32 * ND, 1...]
    pallas_call x1, Pallas kernels: 44.9 us -> 34.6 us  [node(): pl.pallas_call(node_kernel, out_shape=[jax.ShapeDtypeStruct((ND, 256), BF...]
    unnamed x24 -> x14, local copies, waits for them, and re-layouts: 5.78 us -> 1.61 us
    pallas_call x1, Pallas kernels: 28.2 us -> 32 us  [scatter_rows(): pl.pallas_call(scatter_kernel, out_shape=[jax.ShapeDtypeStruct((ND, 128),...]
where the time goes in v2:
time: 113 us
  Pallas kernels  110 us (97%)
  local copies, waits for them, and re-layouts  1.61 us (1%)
  between operations  1.4 us (1%)
    pallas_call x1, Pallas kernels, node(): pl.pallas_call(node_kernel, out_shape=[jax.ShapeDtypeStruct((ND, 256), BF...  34.6 us
    pallas_call x1, Pallas kernels, scatter_rows(): pl.pallas_call(scatter_kernel, out_shape=[jax.ShapeDtypeStruct((ND, 128),...  32 us
    pallas_call x1, Pallas kernels, gather_rows(): pl.pallas_call(gather_kernel, out_shape=[jax.ShapeDtypeStruct((32 * ND, 1...  31 us
    pallas_call x1, Pallas kernels, backward(): pl.pallas_call(backward_kernel, out_shape=[jax.ShapeDtypeStruct((32 * ND,...  6.09 us
    pallas_call x1, Pallas kernels, forward(): pl.pallas_call(functools.partial(spread_kernel, 1, 2), out_shape=jax.Shap...  5.38 us

profile of v2, /device:TPU:1, one launch (start us, length us, event | category | flops | bytes accessed | tf_op | source)
XLA Modules:
  0.0 112.8 jit_solution(26576361909588295)
XLA Ops:
  1.3 0.0 copy-start
  1.3 0.9 copy-done
  2.2 0.0 copy-start.4
  2.2 0.7 copy-done.4
  2.9 0.0 copy-start.5
  2.9 31.0 %gather_rows.1 = (bf16[16384,128]{1,0:T(8,128)(2,1)S(1)}, bf16[128,128,128]{2,1,0:T(8,128)(2,1)S(1)}, f32[64,128]{1,0:T(8,128)S(1)}) custom-call(s32[1]{0:T(128)} %bitcast.6.cnt, s32[1,512]{1,0:T(1,128)S(1)} %bitcast.9, bf16[512,128]{1,0:T(8,128)(2,1)S(1)} %copy-done, s32[512,4096]{1,0:T(8,128)} %bitcast.15), custom_call_target="tpu_custom_call" | custom-call | tf_op jit(solution)/shard_map/gather_rows/pallas_call | solution.py:231
  33.9 0.0 copy-done.5
  33.9 0.0 copy-start.1
  33.9 0.0 copy-start.2
  33.9 0.0 copy-start.3
  33.9 0.0 copy-start.6
  33.9 5.4 %forward.1.raw_part = bf16[4096,128]{1,0:T(8,128)(2,1)S(1)} custom-call(s32[1]{0:T(128)} %bitcast.7.cnt, s32[512]{0:T(512)S(1)} %bitcast.12, s32[512]{0:T(512)S(1)} %bitcast.10, bf16[128,128,128]{2,1,0:T(8,128)(2,1)S(1)} %get-tuple-element.20.blocks.zf, bf16[16384,128]{1,0:T(8,128)(2,1)S(1)} %get-tuple-element.21.table), custom_call_target="tpu_custom_call" | custom-call | tf_op jit(solution)/shard_map/forward/pallas_call | solution.py:291
  39.3 0.0 copy-done.1
  39.3 0.0 copy-done.2
  39.4 0.0 copy-done.3
  39.4 0.0 copy-done.6
  39.4 34.6 %node.1 = (bf16[512,256]{1,0:T(8,128)(2,1)S(1)}, bf16[4096,128]{1,0:T(8,128)(2,1)S(1)}, f32[512,128]{1,0:T(8,128)S(1)}, f32[64,128]{1,0:T(8,128)S(1)}, bf16[128,128,128]{2,1,0:T(8,128)(2,1)S(1)}) custom-call(bf16[4096,128]{1,0:T(8,128)(2,1)S(1)} %forward.1.raw_part, f32[64,128]{1,0:T(8,128)S(1)} %get-tuple-element.22.deg, bf16[512,128]{1,0:T(8,128)(2,1)S(1)} %copy-done, ...), custom_call_target="tpu_custom_call" | custom-call | tf_op jit(solution)/shard_map/node/pallas_call | solution.py:470
  74.0 6.1 %backward.1 = (bf16[16384,128]{1,0:T(8,128)(2,1)S(1)}, bf16[512,256]{1,0:T(8,128)(2,1)}) custom-call(s32[1]{0:T(128)} %bitcast.8.cnt, s32[512]{0:T(512)S(1)} %bitcast.11, s32[512]{0:T(512)S(1)} %bitcast.13, bf16[128,128,128]{2,1,0:T(8,128)(2,1)S(1)} %get-tuple-element.23.blocks, bf16[4096,128]{1,0:T(8,128)(2,1)S(1)} %get-tuple-element.24.table, ...), custom_call_target="tpu_custom_call" | custom-call | tf_op jit(solution)/shard_map/backward/pallas_call | solution.py:310
  80.1 32.0 %scatter_rows.1 = (bf16[512,128]{1,0:T(8,128)(2,1)S(1)}, f32[128,256]{1,0:T(8,128)S(1)}, f32[128,256]{1,0:T(8,128)S(1)}) custom-call(bf16[16384,128]{1,0:T(8,128)(2,1)S(1)} %get-tuple-element.27.t, f32[512,128]{1,0:T(8,128)S(1)} %get-tuple-element.28.own_term, f32[64,128]{1,0:T(8,128)S(1)} %get-tuple-element.29.gpart), custom_call_target="tpu_custom_call" | custom-call | tf_op jit(solution)/shard_map/scatter_rows/pallas_call | solution.py:636
  112.1 0.8 finish.1
Async XLA Ops:
  1.3 0.9 copy-start
  2.2 0.7 copy-start.4
  2.9 31.0 %copy-start.5 = (s32[1,1,512]{2,1,0:T(1,128)S(1)}, s32[1,1,512]{2,1,0:T(1,128)}, u32[]{:S(2)}) copy-start(s32[1,1,512]{2,1,0:T(1,128)} %param.13) | copy-start | bytes 6148
  33.9 5.4 %copy-start.1 = (bf16[512,256]{1,0:T(8,128)(2,1)S(1)}, bf16[512,256]{1,0:T(8,128)(2,1)}, u32[]{:S(2)}) copy-start(bf16[512,256]{1,0:T(8,128)(2,1)} %cot.1) | copy-start | bytes 786436
  33.9 5.4 %copy-start.2 = (bf16[128,256]{1,0:T(8,128)(2,1)S(1)}, bf16[128,256]{1,0:T(8,128)(2,1)}, u32[]{:S(2)}) copy-start(bf16[128,256]{1,0:T(8,128)(2,1)} %ws.1) | copy-start | bytes 196612
  33.9 5.4 %copy-start.3 = (bf16[128,256]{1,0:T(8,128)(2,1)S(1)}, bf16[128,256]{1,0:T(8,128)(2,1)}, u32[]{:S(2)}) copy-start(bf16[128,256]{1,0:T(8,128)(2,1)} %wn.1) | copy-start | bytes 196612
  33.9 5.4 %copy-start.6 = (s32[512]{0:T(512)S(1)}, s32[512]{0:T(512)}, u32[]{:S(2)}) copy-start(s32[512]{0:T(512)} %param.16) | copy-start | bytes 6148

commit v3 on v2

--- a/solution.py
+++ b/solution.py
@@ -16,7 +16,7 @@
 ND = 512
 UNROLL = 16
 WORK = (8, 3, 3, 2, 2)
-TURN = (32, 32, 24)
+TURN = (48, 8)
 
 
 def place():
@@ -72,7 +72,6 @@
     first.wait_recv()
     for d in range(2):
         last[d, 1, 2] = go(table, partner, 0, 256, zs.at[d, 0, 2], along[d])
-    share(table, partner, 0, 256)
     for step in range(1, half + 1):
         arriving, crossing = crossing, []
         for part in (1, 2, 0):
@@ -92,14 +91,45 @@
                 if part == 1:
                     cp = go(table, row, 256, 256, ys.at[2 * step + d], across)
                     crossing.append((cp, base(e, 1)))
-                share(table, row, lo, n)
+                if step == half:
+                    share(table, row, lo, n)
+                elif part == 0:
+                    share(table, row, 0, 512)
                 idle(step)
         for cp, row in arriving:
             cp.wait_recv()
-            share(table, row, 256, 256)
+            share(table, row, 0, 512)
     for cp, row in crossing:
         cp.wait_recv()
         share(table, row, 256, 256)
+
+
+def star_gather(x, table, base, send, xs, ys, along, across, idle):
+    def go(src, row, lo, sem, target):
+        return send(
+            x.at[pl.ds(lo, 256)] if src is x else table.at[pl.ds(row + lo, 256)],
+            table.at[pl.ds(row + lo, 256)],
+            sem,
+            target,
+        )
+
+    own, partner = base(0, 0), base(0, 1)
+    idle("B")
+    second = [go(x, own, 256, xs.at[e - 1, 1], along[e]) for e in (1, 3, 2)]
+    rest = [go(x, own, 256, ys.at[0], across)]
+    idle("A")
+    first = go(x, own, 0, ys.at[4], across)
+    rest += [go(x, own, 0, xs.at[e - 1, 0], along[e]) for e in (1, 3, 2)]
+    idle("sent")
+    first.wait_recv()
+    rest += [go(table, partner, 0, xs.at[e - 1, 2], along[e]) for e in (1, 3, 2)]
+    idle("partner")
+    for cp, e in zip(second, (1, 3, 2)):
+        cp.wait_recv()
+        rest.append(go(table, base(4 - e, 0), 256, ys.at[e], across))
+    idle("last")
+    for cp in rest:
+        cp.wait_recv()
 
 
 def ring_reduce(half, value, direct, zsrc, rz, send, zs, along):
@@ -139,9 +169,9 @@
 
 
 def gather_kernel(
-    cnt, rows, x, w,
+    cnt, rows_hbm, x, w,
     g, zf, deg,
-    wv, pat, dsl, ss, zs, ys, ks, ls, wsem,
+    wv, rows, pat, dsl, ss, zs, ys, ks, ls, wsem,
 ):
     z, yl, k, col = place()
 
@@ -152,6 +182,8 @@
     for i in range(8):
         slabs.append(pltpu.make_async_copy(w.at[pl.ds(i * 64, 64)], wv.at[pl.ds(i * 64, 64)], wsem.at[i]))
         slabs[-1].start()
+    names = pltpu.make_async_copy(rows_hbm, rows, ls.at[1])
+    names.start()
     along = (dev(lax.rem(z + 1, 8), yl, k), dev(lax.rem(z + 7, 8), yl, k))
     across, sibling = dev(z, 1 - yl, k), dev(z, yl, 1 - k)
     greet((*along, across, sibling))
@@ -213,10 +245,11 @@
             pat[...] = (at == lax.broadcasted_iota(jnp.int32, (4096, 128), 1)).astype(BF)
         idle(step)
 
-    mine = pltpu.make_async_copy(x, g.at[pl.ds(base(0, 0), ND)], ls)
+    mine = pltpu.make_async_copy(x, g.at[pl.ds(base(0, 0), ND)], ls.at[0])
     mine.start()
     ring_gather(4, x, g, base, send, zs, ys, along, across, share, prepare)
     work(64)
+    names.wait()
     slot = lax.broadcasted_iota(jnp.int32, (64, 512), 1)
     hot = (lax.broadcasted_iota(jnp.int32, (64, 512), 0) == rows[...]) & (slot < lim)
     deg[...] = jnp.dot(hot.astype(F32).astype(BF), dsl[...], preferred_element_type=F32)
@@ -228,6 +261,9 @@
 
 
 def gather_rows(count, rows, x, w):
+    rows = pltpu.with_memory_space_constraint(rows, pltpu.HBM)
+    x = pltpu.with_memory_space_constraint(x, pltpu.HBM)
+    w = pltpu.with_memory_space_constraint(w, pltpu.HBM)
     return pl.pallas_call(
         gather_kernel,
         out_shape=[
@@ -235,17 +271,18 @@
             jax.ShapeDtypeStruct((128, 128, 128), BF),
             jax.ShapeDtypeStruct((64, 128), F32),
         ],
-        in_specs=[SMEM, VMEM, ANY, pl.BlockSpec(memory_space=pltpu.HBM)],
+        in_specs=[SMEM, ANY, ANY, ANY],
         out_specs=[ANY, VMEM, VMEM],
         scratch_shapes=[
             pltpu.VMEM((512, 4096), jnp.int32),
+            pltpu.VMEM((1, 512), jnp.int32),
             pltpu.VMEM((4096, 128), BF),
             pltpu.VMEM((512, 128), BF),
             pltpu.SemaphoreType.DMA((80,)),
             pltpu.SemaphoreType.DMA((2, 4, 3)),
             pltpu.SemaphoreType.DMA((10,)),
             pltpu.SemaphoreType.DMA((40,)),
-            pltpu.SemaphoreType.DMA,
+            pltpu.SemaphoreType.DMA((2,)),
             pltpu.SemaphoreType.DMA((8,)),
         ],
         compiler_params=pltpu.CompilerParams(
@@ -337,7 +374,7 @@
 def node_kernel(
     raw_part, deg, x, ws, wn, mask, cot, zf,
     hidden, group, own_term, gsum, zt,
-    yb, zsrc, rz, fsrc, fy, rd, nat, sc, grads, gr, ss, z1, y1, z2, y2, ds, gsem, ls,
+    yb, xsrc, rx, fsrc, fy, rd, nat, sc, grads, gr, ss, x1, y1, x2, y2, ds, gsem, ls,
 ):
     row, col = lax.axis_index("row"), lax.axis_index("col")
     yh, xx = col // 4, lax.rem(col, 4)
@@ -345,7 +382,7 @@
     zat = [lax.rem(z + e, 8) for e in range(8)]
     xat = [lax.rem(xx + e, 4) for e in range(4)]
     peers = [lax.rem(col + o, 8) for o in range(8)]
-    up, down = (row, yh * 4 + xat[1]), (row, yh * 4 + xat[3])
+    along = [(row, yh * 4 + xat[e]) for e in range(4)]
     across = (row, (1 - yh) * 4 + xx)
     greet([(row, p) for p in peers[1:]] + [(zat[e] * 4 + side, col) for e in range(1, 8)])
     send, sent = sender(ss)
@@ -353,109 +390,112 @@
     def base(e, r):
         return pl.multiple_of(((yh if r == 0 else 1 - yh) * 4 + xat[e]) * ND, ND)
 
-    def part_ref(e, part, lo, n):
-        row0 = base(e, 1 if part == 2 else 0) + (256 if part == 1 else 0)
-        return raw_part.at[pl.ds(row0 + lo, n)]
-
-    ysent = {}
-
-    def cross(e):
-        ysent[e] = send(raw_part.at[pl.ds(base(e, 1) + 256, 256)], yb.at[e], y1.at[e], across)
-
-    crossed = set()
-
-    def value(e, part, lo, n):
-        total = part_ref(e, part, lo, n)[...].astype(F32)
-        if part == 1:
-            if e not in crossed:
-                ysent[e].wait_recv()
-                crossed.add(e)
-            total = total + yb[e, lo : lo + n, :].astype(F32)
-        return total
-
-    def direct(e, part, lo, n):
-        return None if part == 1 else part_ref(e, part, lo, n)
-
-    piece, final = ring_reduce(2, value, direct, zsrc, rz, send, z1, (down, up))
-
-    def turn(lo, n):
-        @pl.loop(lo, lo + n)
-        def _(i):
-            zt[i] = zf[i].T
-
-    cross(2)
-    piece(0, 2, 2)
-    piece(1, 2, 2)
-    piece(0, 2, 0)
-    cross(1)
-    cross(3)
-    piece(1, 1, 0)
-    cross(0)
-    rd[0] = deg[pl.ds(pl.multiple_of(col * 8, 8), 8), :]
+    def mine(e, r, lo):
+        return raw_part.at[pl.ds(base(e, r) + lo, 256)]
+
+    ysent = {e: send(mine(e, 1, 256), yb.at[e], y1.at[e], across) for e in (2, 1, 3)}
+    xsent = {}
+    for part in (2, 0):
+        for e in (2, 1, 3):
+            src = mine(e, 1 if part == 2 else 0, 0)
+            xsent[e, part] = send(src, rx.at[e - 1, part], x1.at[e - 1, part], along[e])
+            if part == 2 and e == 2:
+                ysent[0] = send(mine(0, 1, 256), yb.at[0], y1.at[0], across)
     degs = []
     for o in range(1, 8):
         src = deg.at[pl.ds(pl.multiple_of(peers[o] * 8, 8), 8)]
         degs.append(send(src, rd.at[o], ds.at[o], (row, peers[o])))
-    feats = x[...]
-    pre_self = jnp.dot(feats, ws[...], preferred_element_type=F32)
+
+    def pass_on(e):
+        ysent[e].wait_recv()
+        xsrc[e - 1] = (mine(e, 0, 256)[...].astype(F32) + yb[e].astype(F32)).astype(BF)
+        xsent[e, 1] = send(xsrc.at[e - 1], rx.at[e - 1, 1], x1.at[e - 1, 1], along[e])
+
+    def final(part, total):
+        for e in (2, 1, 3):
+            xsent[e, part].wait_recv()
+            total = total + rx[e - 1, part].astype(F32)
+        return total
+
+    pass_on(2)
+    pass_on(1)
+    pass_on(3)
+    fsrc[...] = final(2, mine(0, 1, 0)[...].astype(F32)).astype(BF)
+    last = send(fsrc, fy, y1.at[4], across)
+    rd[0] = deg[pl.ds(pl.multiple_of(col * 8, 8), 8), :]
     keep = upright(mask[...].astype(F32), 128)
-    turn(0, TURN[0])
-    piece(1, 2, 1)
-    piece(0, 1, 1)
-    piece(0, 1, 2)
-    piece(1, 1, 2)
-    piece(0, 1, 0)
-    piece(1, 1, 1)
     for cp in degs:
         cp.wait_recv()
-    degree = upright(jnp.sum(rd[...], axis=0), 64)
-    turn(TURN[0], TURN[1])
-    fsrc[...] = final(2).astype(BF)
-    last = send(fsrc, fy, y1.at[4], across)
-    second = final(1)
-    first = final(0)
-    turn(TURN[0] + TURN[1], TURN[2])
-    last.wait_recv()
-    raw = jnp.concatenate([first + fy[...].astype(F32), second], 0).reshape(8, 2, 32, 128)
-    for p in range(2):
-        nat[pl.ds(p, 256, stride=2), :] = raw[:, p].reshape(256, 128)
-    agg = (nat[...] / degree).astype(BF)
-    pre = pre_self + jnp.dot(agg, wn[...], preferred_element_type=F32)
-    sig = jax.nn.sigmoid(pre)
-    dpre = (cot[...].astype(F32) * keep * sig * (1.0 + pre * (1.0 - sig))).astype(BF)
+    inverse = 1.0 / upright(jnp.sum(rd[...], axis=0), 64)
     nt = (((1,), (1,)), ((), ()))
     tn = (((0,), (0,)), ((), ()))
-    nat[...] = lax.dot_general(dpre, wn[...], nt, preferred_element_type=F32) / degree
-    for p in range(2):
-        part = nat[pl.ds(p, 256, stride=2), :].astype(BF).reshape(8, 32, 128)
-        for i in range(8):
-            sc[i * 64 + p * 32 : i * 64 + p * 32 + 32, :] = part[i]
-    stay = pltpu.make_async_copy(sc, group.at[pl.ds(base(0, 0), ND)], ls)
-    stay.start()
-    todo = []
+    halves = {}
+
+    def layer(lo, raw):
+        at = pl.ds(lo, 256)
+        raw = raw.reshape(4, 2, 32, 128)
+        for p in range(2):
+            nat[pl.ds(lo + p, 128, stride=2), :] = raw[:, p].reshape(128, 128)
+        inv = inverse[lo : lo + 256]
+        agg = (nat[at, :] * inv).astype(BF)
+        feats = x[at, :]
+        pre = jnp.dot(feats, ws[...], preferred_element_type=F32)
+        pre = pre + jnp.dot(agg, wn[...], preferred_element_type=F32)
+        sig = jax.nn.sigmoid(pre)
+        slope = sig * (1.0 + pre * (1.0 - sig))
+        dpre = (cot[at, :].astype(F32) * keep[lo : lo + 256] * slope).astype(BF)
+        nat[at, :] = lax.dot_general(dpre, wn[...], nt, preferred_element_type=F32) * inv
+        for p in range(2):
+            part = nat[pl.ds(lo + p, 128, stride=2), :].astype(BF).reshape(4, 32, 128)
+            for i in range(4):
+                sc[lo + i * 64 + p * 32 : lo + i * 64 + p * 32 + 32, :] = part[i]
+        hidden[at, :] = (pre * sig).astype(BF)
+        halves[lo] = feats, agg, dpre
+
     slices = []
 
     def later():
-        hidden[...] = (pre * sig).astype(BF)
-        own_term[...] = lax.dot_general(dpre, ws[...], nt, preferred_element_type=F32)
-        g_self = lax.dot_general(feats, dpre, tn, preferred_element_type=F32)
-        g_neigh = lax.dot_general(agg, dpre, tn, preferred_element_type=F32)
+        g_self, g_neigh = 0.0, 0.0
+        for lo, (feats, agg, dpre) in halves.items():
+            own_term[lo : lo + 256, :] = lax.dot_general(dpre, ws[...], nt, preferred_element_type=F32)
+            g_self = g_self + lax.dot_general(feats, dpre, tn, preferred_element_type=F32)
+            g_neigh = g_neigh + lax.dot_general(agg, dpre, tn, preferred_element_type=F32)
         for i, v in enumerate((g_self[:, :128], g_self[:, 128:], g_neigh[:, :128], g_neigh[:, 128:])):
             grads[i * 128 : i * 128 + 128, :] = v
         for e in range(1, 8):
             src = grads.at[pl.ds(pl.multiple_of(zat[e] * 64, 64), 64)]
             slices.append(send(src, gr.at[e], gsem.at[e], (zat[e] * 4 + side, col)))
 
-    def idle(step):
-        if step == 0:
+    turned = [0]
+
+    def turn(n):
+        lo = turned[0]
+        turned[0] += n
+
+        @pl.loop(lo, lo + n)
+        def _(i):
+            zt[i] = zf[i].T
+
+    stay = pltpu.make_async_copy(sc, group.at[pl.ds(base(0, 0), ND)], ls)
+
+    def idle(when):
+        if when == "B":
+            ysent[0].wait_recv()
+            layer(256, final(1, mine(0, 0, 256)[...].astype(F32) + yb[0].astype(F32)))
+        elif when == "A":
+            first = final(0, mine(0, 0, 0)[...].astype(F32))
+            last.wait_recv()
+            layer(0, first + fy[...].astype(F32))
+        elif when == "sent":
+            stay.start()
+            turn(TURN[0])
+        elif when == "partner":
+            turn(TURN[1])
+        else:
             later()
-        elif not todo:
-            todo.append(1)
-            turn(sum(TURN[:3]), 128 - sum(TURN[:3]))
-
-    ring_gather(
-        2, sc, group, base, send, z2, y2, (up, down), across, lambda *a: None, idle
-    )
+            turn(128 - TURN[0] - TURN[1])
+
+    star_gather(sc, group, base, send, x2, y2, along, across, idle)
     total = grads[pl.ds(pl.multiple_of(z * 64, 64), 64), :]
     for e in range(1, 8):
         slices[e - 1].wait_recv()
@@ -480,8 +520,8 @@
         out_specs=[VMEM, ANY, VMEM, VMEM, VMEM],
         scratch_shapes=[
             pltpu.VMEM((4, 256, 128), BF),
-            pltpu.VMEM((2, 2, 768, 128), BF),
-            pltpu.VMEM((2, 2, 768, 128), BF),
+            pltpu.VMEM((3, 256, 128), BF),
+            pltpu.VMEM((3, 3, 256, 128), BF),
             pltpu.VMEM((256, 128), BF),
             pltpu.VMEM((256, 128), BF),
             pltpu.VMEM((8, 8, 128), F32),
@@ -490,10 +530,10 @@
             pltpu.VMEM((512, 128), F32),
             pltpu.VMEM((8, 64, 128), F32),
             pltpu.SemaphoreType.DMA((60,)),
-            pltpu.SemaphoreType.DMA((2, 2, 3)),
+            pltpu.SemaphoreType.DMA((3, 3)),
             pltpu.SemaphoreType.DMA((5,)),
-            pltpu.SemaphoreType.DMA((2, 2, 3)),
-            pltpu.SemaphoreType.DMA((6,)),
+            pltpu.SemaphoreType.DMA((3, 3)),
+            pltpu.SemaphoreType.DMA((5,)),
             pltpu.SemaphoreType.DMA((8,)),
             pltpu.SemaphoreType.DMA((8,)),
             pltpu.SemaphoreType.DMA,
@@ -516,8 +556,8 @@
 def scatter_kernel(
     t, own_term, gpart,
     out, grad_self, grad_neigh,
-    own, sib, ysrc, yb, zsrc, rz, fsrc, fy, gk, gx, gy, gsrc, gall,
-    ss, zs, ys, ks, ls, q0, q1, q2, q3,
+    sib, ysrc, yb, zsrc, rz, fsrc, fy, gk, gx, gy, gsrc, gall,
+    ss, zs, ys, ks, q0, q1, q2, q3,
 ):
     z, yl, k, col = place()
 
@@ -538,24 +578,18 @@
     ours = pl.ds(pl.multiple_of(k * 32, 32), 32)
     halves = send(gpart.at[theirs], gk, q0.at[0], sibling)
 
-    loads, sibs = {}, {}
+    sibs = {}
     for e in (4, 3, 5, 2, 6, 1, 7, 0):
-        for r in (1, 0):
-            yy = yl if r == 0 else 1 - yl
-            row = (zat[e] * 4 + yy * 2) * ND
-            theirs = pl.ds(pl.multiple_of(row + (1 - k) * ND, ND), ND)
-            ours = pl.ds(pl.multiple_of(row + k * ND, ND), ND)
-            sibs[e, r] = send(t.at[theirs], sib.at[e, r], ks.at[e, r], sibling)
-            loads[e, r] = pltpu.make_async_copy(t.at[ours], own.at[e, r], ls.at[e, r])
-            loads[e, r].start()
+        sibs[e] = send(t.at[zat[e], :, 1 - k], sib.at[e], ks.at[e], sibling)
     ready = set()
 
     def mine(e, r, lo, n):
-        if (e, r) not in ready:
-            loads[e, r].wait()
-            sibs[e, r].wait_recv()
-            ready.add((e, r))
-        return own[e, r, lo : lo + n, :].astype(F32) + sib[e, r, lo : lo + n, :].astype(F32)
+        if e not in ready:
+            sibs[e].wait_recv()
+            ready.add(e)
+        yy = yl if r == 0 else 1 - yl
+        at = pl.ds(lo, n)
+        return t[zat[e], yy, k, at, :].astype(F32) + sib[e, yy, at, :].astype(F32)
 
     ysent = {}
 
@@ -640,10 +674,9 @@
             jax.ShapeDtypeStruct((128, 256), F32),
             jax.ShapeDtypeStruct((128, 256), F32),
         ],
-        in_specs=[ANY, VMEM, VMEM],
+        in_specs=[VMEM, VMEM, VMEM],
         out_specs=[VMEM, VMEM, VMEM],
         scratch_shapes=[
-            pltpu.VMEM((8, 2, ND, 128), BF),
             pltpu.VMEM((8, 2, ND, 128), BF),
             pltpu.VMEM((8, 256, 128), BF),
             pltpu.VMEM((8, 256, 128), BF),
@@ -659,8 +692,7 @@
             pltpu.SemaphoreType.DMA((90,)),
             pltpu.SemaphoreType.DMA((2, 4, 3)),
             pltpu.SemaphoreType.DMA((9,)),
-            pltpu.SemaphoreType.DMA((8, 2)),
-            pltpu.SemaphoreType.DMA((8, 2)),
+            pltpu.SemaphoreType.DMA((8,)),
             pltpu.SemaphoreType.DMA((2,)),
             pltpu.SemaphoreType.DMA((3,)),
             pltpu.SemaphoreType.DMA((3,)),
@@ -670,7 +702,7 @@
             collective_id=2, has_side_effects=True, vmem_limit_bytes=20 << 20
         ),
         name="scatter_rows",
-    )(t, own_term, grads)
+    )(t.reshape(8, 2, 2, ND, 128), own_term, grads)
 
 
 def finish_kernel(*refs):

time: 113 us -> 106 us (0.938)
  Pallas kernels: 110 us -> 104 us
  local copies, waits for them, and re-layouts: 1.61 us -> 0.04 us
    pallas_call x1, Pallas kernels: 5.38 us -> 2.52 us  [forward(): pl.pallas_call(functools.partial(spread_kernel, 1, 2), out_shape=jax.Shap...]
    pallas_call x1, Pallas kernels: 6.09 us -> 3.25 us  [backward(): pl.pallas_call(backward_kernel, out_shape=[jax.ShapeDtypeStruct((32 * ND,...]
    pallas_call x1, Pallas kernels: 34.6 us -> 32.1 us  [node(): pl.pallas_call(node_kernel, out_shape=[jax.ShapeDtypeStruct((ND, 256), BF...]
    pallas_call x1, Pallas kernels: 32 us -> 34.1 us  [scatter_rows(): pl.pallas_call(scatter_kernel, out_shape=[jax.ShapeDtypeStruct((ND, 128),...]
    unnamed x14, local copies, waits for them, and re-layouts: 1.61 us -> 0.04 us
where the time goes in v3:
time: 106 us
  Pallas kernels  104 us (98%)
  between operations  1.43 us (1%)
    pallas_call x1, Pallas kernels, scatter_rows(): pl.pallas_call(scatter_kernel, out_shape=[jax.ShapeDtypeStruct((ND, 128),...  34.1 us
    pallas_call x1, Pallas kernels, node(): pl.pallas_call(node_kernel, out_shape=[jax.ShapeDtypeStruct((ND, 256), BF...  32.1 us
    pallas_call x1, Pallas kernels, gather_rows(): pl.pallas_call(gather_kernel, out_shape=[jax.ShapeDtypeStruct((32 * ND, 1...  31.5 us
    pallas_call x1, Pallas kernels, backward(): pl.pallas_call(backward_kernel, out_shape=[jax.ShapeDtypeStruct((32 * ND,...  3.25 us
    pallas_call x1, Pallas kernels, forward(): pl.pallas_call(functools.partial(spread_kernel, 1, 2), out_shape=jax.Shap...  2.52 us

profile of v3, /device:TPU:1, one launch (start us, length us, event | category | flops | bytes accessed | tf_op | source)
XLA Modules:
  0.0 105.6 jit_solution(15698147511868478049)
XLA Ops:
  1.3 0.0 copy-start.4
  1.3 0.0 copy-start.5
  1.3 31.5 %gather_rows.1 = (bf16[16384,128]{1,0:T(8,128)(2,1)S(1)}, bf16[128,128,128]{2,1,0:T(8,128)(2,1)S(1)}, f32[64,128]{1,0:T(8,128)S(1)}) custom-call(s32[1]{0:T(128)} %bitcast.7.cnt, s32[1,512]{1,0:T(1,128)} %bitcast.11, bf16[512,128]{1,0:T(8,128)(2,1)} %x.3, s32[512,4096]{1,0:T(8,128)} %bitcast.17), custom_call_target="tpu_custom_call" | custom-call | tf_op jit(solution)/shard_map/gather_rows/pallas_call | solution.py:267
  32.8 0.0 copy-done.4
  32.8 0.0 copy-done.5
  32.8 0.0 copy-start
  32.8 0.0 copy-start.1
  32.8 0.0 copy-start.2
  32.8 0.0 copy-start.3
  32.9 0.0 copy-start.6
  32.9 2.5 %forward.1.raw_part = bf16[4096,128]{1,0:T(8,128)(2,1)S(1)} custom-call(s32[1]{0:T(128)} %bitcast.8.cnt, s32[512]{0:T(512)S(1)} %bitcast.14, s32[512]{0:T(512)S(1)} %bitcast.12, bf16[128,128,128]{2,1,0:T(8,128)(2,1)S(1)} %get-tuple-element.20.blocks.zf, bf16[16384,128]{1,0:T(8,128)(2,1)S(1)} %get-tuple-element.21.table), custom_call_target="tpu_custom_call" | custom-call | tf_op jit(solution)/shard_map/forward/pallas_call | solution.py:328
  35.4 0.0 copy-done
  35.4 0.0 copy-done.1
  35.4 0.0 copy-done.2
  35.4 0.0 copy-done.3
  35.4 0.0 copy-done.6
  35.4 32.1 %node.1 = (bf16[512,256]{1,0:T(8,128)(2,1)S(1)}, bf16[4096,128]{1,0:T(8,128)(2,1)S(1)}, f32[512,128]{1,0:T(8,128)S(1)}, f32[64,128]{1,0:T(8,128)S(1)}, bf16[128,128,128]{2,1,0:T(8,128)(2,1)S(1)}) custom-call(bf16[4096,128]{1,0:T(8,128)(2,1)S(1)} %forward.1.raw_part, f32[64,128]{1,0:T(8,128)S(1)} %get-tuple-element.22.deg, bf16[512,128]{1,0:T(8,128)(2,1)S(1)} %copy-done, ...), custom_call_target="tpu_custom_call" | custom-call | tf_op jit(solution)/shard_map/node/pallas_call | solution.py:510
  67.5 3.3 %backward.1 = (bf16[16384,128]{1,0:T(8,128)(2,1)S(1)}, bf16[512,256]{1,0:T(8,128)(2,1)}) custom-call(s32[1]{0:T(128)} %bitcast.9.cnt, s32[512]{0:T(512)S(1)} %bitcast.13, s32[512]{0:T(512)S(1)} %bitcast.15, bf16[128,128,128]{2,1,0:T(8,128)(2,1)S(1)} %get-tuple-element.23.blocks, bf16[4096,128]{1,0:T(8,128)(2,1)S(1)} %get-tuple-element.24.table, ...), custom_call_target="tpu_custom_call" | custom-call | tf_op jit(solution)/shard_map/backward/pallas_call | solution.py:347
  70.8 34.1 %scatter_rows.1 = (bf16[512,128]{1,0:T(8,128)(2,1)S(1)}, f32[128,256]{1,0:T(8,128)S(1)}, f32[128,256]{1,0:T(8,128)S(1)}) custom-call(bf16[8,2,2,512,128]{4,3,2,1,0:T(8,128)(2,1)S(1)} %bitcast.10, f32[512,128]{1,0:T(8,128)S(1)} %get-tuple-element.28.own_term, f32[64,128]{1,0:T(8,128)S(1)} %get-tuple-element.29.gpart), custom_call_target="tpu_custom_call" | custom-call | tf_op jit(solution)/shard_map/scatter_rows/pallas_call | solution.py:670
  104.9 0.8 finish.1
Async XLA Ops:
  1.3 31.5 %copy-start.4 = (s32[1,1,512]{2,1,0:T(1,128)S(1)}, s32[1,1,512]{2,1,0:T(1,128)}, u32[]{:S(2)}) copy-start(s32[1,1,512]{2,1,0:T(1,128)} %param.12) | copy-start | bytes 6148
  1.3 31.5 %copy-start.5 = (s32[1,1,512]{2,1,0:T(1,128)S(1)}, s32[1,1,512]{2,1,0:T(1,128)}, u32[]{:S(2)}) copy-start(s32[1,1,512]{2,1,0:T(1,128)} %param.13) | copy-start | bytes 6148
  32.8 2.6 %copy-start = (bf16[512,128]{1,0:T(8,128)(2,1)S(1)}, bf16[512,128]{1,0:T(8,128)(2,1)}, u32[]{:S(2)}) copy-start(bf16[512,128]{1,0:T(8,128)(2,1)} %x.3) | copy-start | bytes 393220
  32.8 2.6 %copy-start.1 = (bf16[512,256]{1,0:T(8,128)(2,1)S(1)}, bf16[512,256]{1,0:T(8,128)(2,1)}, u32[]{:S(2)}) copy-start(bf16[512,256]{1,0:T(8,128)(2,1)} %cot.1) | copy-start | bytes 786436
  32.8 2.6 %copy-start.2 = (bf16[128,256]{1,0:T(8,128)(2,1)S(1)}, bf16[128,256]{1,0:T(8,128)(2,1)}, u32[]{:S(2)}) copy-start(bf16[128,256]{1,0:T(8,128)(2,1)} %ws.1) | copy-start | bytes 196612
  32.8 2.6 %copy-start.3 = (bf16[128,256]{1,0:T(8,128)(2,1)S(1)}, bf16[128,256]{1,0:T(8,128)(2,1)}, u32[]{:S(2)}) copy-start(bf16[128,256]{1,0:T(8,128)(2,1)} %wn.1) | copy-start | bytes 196612
  32.9 2.6 %copy-start.6 = (s32[512]{0:T(512)S(1)}, s32[512]{0:T(512)}, u32[]{:S(2)}) copy-start(s32[512]{0:T(512)} %param.16) | copy-start | bytes 6148

commit v4 on v3

--- a/solution.py
+++ b/solution.py
@@ -14,9 +14,9 @@
 SMEM = pl.BlockSpec(memory_space=pltpu.SMEM)
 ANY = pl.BlockSpec(memory_space=pl.ANY)
 ND = 512
-UNROLL = 16
-WORK = (8, 3, 3, 2, 2)
-TURN = (48, 8)
+UNROLL = 32
+WORK = (8, 3, 3, 3, 1)
+TURN = (32,)
 
 
 def place():
@@ -24,10 +24,12 @@
     return row // 4, (row // 2) % 2, row % 2, lax.axis_index("col")
 
 
-def greet(targets):
+def greet(targets, meanwhile=None):
     barrier = pltpu.get_barrier_semaphore()
     for target in targets:
         pl.semaphore_signal(barrier, inc=1, device_id=target, device_id_type=MESH)
+    if meanwhile is not None:
+        meanwhile()
     pl.semaphore_wait(barrier, len(targets))
 
 
@@ -62,46 +64,55 @@
         )
 
     own, partner = base(0, 0), base(0, 1)
-    first = go(x, own, 0, 256, ys.at[0], across)
+    first = [go(x, own, 128 * i, 128, ys.at[0, i], across) for i in range(2)]
     for part in (1, 0):
-        for d in range(2):
-            last[d, 1, part] = go(x, own, part * 256, 256, zs.at[d, 0, part], along[d])
-    crossing = [(go(x, own, 256, 256, ys.at[1], across), partner)]
+        for i in range(2):
+            for d in range(2):
+                lo = part * 256 + i * 128
+                last[d, 1, part, i] = go(x, own, lo, 128, zs.at[d, 0, part, i], along[d])
+    crossing = [([go(x, own, 256, 256, ys.at[1, 0], across)], partner)]
     share(x, own, 0, 512)
     idle(0)
-    first.wait_recv()
-    for d in range(2):
-        last[d, 1, 2] = go(table, partner, 0, 256, zs.at[d, 0, 2], along[d])
+    for i in range(2):
+        first[i].wait_recv()
+        for d in range(2):
+            last[d, 1, 2, i] = go(table, partner, 128 * i, 128, zs.at[d, 0, 2, i], along[d])
     for step in range(1, half + 1):
         arriving, crossing = crossing, []
-        for part in (1, 2, 0):
+        crossed = ([], [])
+        for part, i in ((1, 0), (1, 1), (2, 0), (2, 1), (0, 0), (0, 1)):
             for d in range(2):
-                if (d, step, part) not in last:
+                if (d, step, part, i) not in last:
                     continue
                 e = 2 * half - step if d == 0 else step
                 row = base(e, 0 if part < 2 else 1)
-                lo, n = (0, 256, 0)[part], 256
-                if step == half and part == 2:
-                    lo, n = d * 128, 128
-                last[d, step, part].wait_recv()
-                if step < half - 1 or (step == half - 1 and part == d):
-                    last[d, step + 1, part] = go(table, row, lo, n, zs.at[d, step, part], along[d])
-                elif step == half - 1 and part == 2:
-                    last[d, half, 2] = go(table, row, d * 128, 128, zs.at[d, step, 2], along[d])
+                lo = (0, 256, 0)[part] + 128 * i
+                last[d, step, part, i].wait_recv()
+                goes = step < half - 1
+                if step == half - 1:
+                    goes = part == d or (part == 2 and i == d)
+                if goes:
+                    last[d, step + 1, part, i] = go(
+                        table, row, lo, 128, zs.at[d, step, part, i], along[d]
+                    )
                 if part == 1:
-                    cp = go(table, row, 256, 256, ys.at[2 * step + d], across)
-                    crossing.append((cp, base(e, 1)))
+                    cp = go(table, row, lo, 128, ys.at[2 * step + d, i], across)
+                    crossed[d].append(cp)
+                    if i == 1:
+                        crossing.append((crossed[d], base(e, 1)))
                 if step == half:
-                    share(table, row, lo, n)
-                elif part == 0:
+                    share(table, row, lo, 128)
+                elif part == 0 and i == 1:
                     share(table, row, 0, 512)
-                idle(step)
-        for cp, row in arriving:
+            idle(step)
+        for cps, row in arriving:
+            for cp in cps:
+                cp.wait_recv()
+            share(table, row, 0, 512)
+    for cps, row in crossing:
+        for i, cp in enumerate(cps):
             cp.wait_recv()
-            share(table, row, 0, 512)
-    for cp, row in crossing:
-        cp.wait_recv()
-        share(table, row, 256, 256)
+            share(table, row, 256 + 128 * i, 128)
 
 
 def star_gather(x, table, base, send, xs, ys, along, across, idle):
@@ -178,15 +189,21 @@
     def dev(zz, yy, kk):
         return (zz * 4 + yy * 2 + kk, col)
 
-    slabs = []
-    for i in range(8):
-        slabs.append(pltpu.make_async_copy(w.at[pl.ds(i * 64, 64)], wv.at[pl.ds(i * 64, 64)], wsem.at[i]))
-        slabs[-1].start()
-    names = pltpu.make_async_copy(rows_hbm, rows, ls.at[1])
-    names.start()
     along = (dev(lax.rem(z + 1, 8), yl, k), dev(lax.rem(z + 7, 8), yl, k))
     across, sibling = dev(z, 1 - yl, k), dev(z, yl, 1 - k)
-    greet((*along, across, sibling))
+    slabs = [
+        pltpu.make_async_copy(w.at[pl.ds(i * 64, 64)], wv.at[pl.ds(i * 64, 64)], wsem.at[i])
+        for i in range(8)
+    ]
+    names = pltpu.make_async_copy(rows_hbm, rows, ls.at[1])
+
+    def fetch():
+        for cp in (*slabs, names):
+            cp.start()
+        at = lax.broadcasted_iota(jnp.int32, (4096, 128), 0) // 64
+        pat[...] = (at == lax.broadcasted_iota(jnp.int32, (4096, 128), 1)).astype(BF)
+
+    greet((*along, across, sibling), fetch)
     send, sent = sender(ss)
 
     def base(e, r):
@@ -239,15 +256,9 @@
     def idle(step):
         work(WORK[step])
 
-    def prepare(step):
-        if step == 0:
-            at = lax.broadcasted_iota(jnp.int32, (4096, 128), 0) // 64
-            pat[...] = (at == lax.broadcasted_iota(jnp.int32, (4096, 128), 1)).astype(BF)
-        idle(step)
-
     mine = pltpu.make_async_copy(x, g.at[pl.ds(base(0, 0), ND)], ls.at[0])
     mine.start()
-    ring_gather(4, x, g, base, send, zs, ys, along, across, share, prepare)
+    ring_gather(4, x, g, base, send, zs, ys, along, across, share, idle)
     work(64)
     names.wait()
     slot = lax.broadcasted_iota(jnp.int32, (64, 512), 1)
@@ -278,9 +289,9 @@
             pltpu.VMEM((1, 512), jnp.int32),
             pltpu.VMEM((4096, 128), BF),
             pltpu.VMEM((512, 128), BF),
-            pltpu.SemaphoreType.DMA((80,)),
-            pltpu.SemaphoreType.DMA((2, 4, 3)),
-            pltpu.SemaphoreType.DMA((10,)),
+            pltpu.SemaphoreType.DMA((110,)),
+            pltpu.SemaphoreType.DMA((2, 4, 3, 2)),
+            pltpu.SemaphoreType.DMA((10, 2)),
             pltpu.SemaphoreType.DMA((40,)),
             pltpu.SemaphoreType.DMA((2,)),
             pltpu.SemaphoreType.DMA((8,)),
@@ -384,7 +395,12 @@
     peers = [lax.rem(col + o, 8) for o in range(8)]
     along = [(row, yh * 4 + xat[e]) for e in range(4)]
     across = (row, (1 - yh) * 4 + xx)
-    greet([(row, p) for p in peers[1:]] + [(zat[e] * 4 + side, col) for e in range(1, 8)])
+    early = []
+
+    def unmask():
+        early.append(upright(mask[...].astype(F32), 128))
+
+    greet([(row, p) for p in peers[1:]] + [(zat[e] * 4 + side, col) for e in range(1, 8)], unmask)
     send, sent = sender(ss)
 
     def base(e, r):
@@ -423,7 +439,7 @@
     fsrc[...] = final(2, mine(0, 1, 0)[...].astype(F32)).astype(BF)
     last = send(fsrc, fy, y1.at[4], across)
     rd[0] = deg[pl.ds(pl.multiple_of(col * 8, 8), 8), :]
-    keep = upright(mask[...].astype(F32), 128)
+    keep = early[0]
     for cp in degs:
         cp.wait_recv()
     inverse = 1.0 / upright(jnp.sum(rd[...], axis=0), 64)
@@ -461,7 +477,7 @@
             g_self = g_self + lax.dot_general(feats, dpre, tn, preferred_element_type=F32)
             g_neigh = g_neigh + lax.dot_general(agg, dpre, tn, preferred_element_type=F32)
         for i, v in enumerate((g_self[:, :128], g_self[:, 128:], g_neigh[:, :128], g_neigh[:, 128:])):
-            grads[i * 128 : i * 128 + 128, :] = v
+            grads[i * 128 : i * 128 + 128, :] = v.astype(BF)
         for e in range(1, 8):
             src = grads.at[pl.ds(pl.multiple_of(zat[e] * 64, 64), 64)]
             slices.append(send(src, gr.at[e], gsem.at[e], (zat[e] * 4 + side, col)))
@@ -488,18 +504,18 @@
             layer(0, first + fy[...].astype(F32))
         elif when == "sent":
             stay.start()
-            turn(TURN[0])
+            turn(48)
         elif when == "partner":
-            turn(TURN[1])
+            turn(8)
         else:
             later()
-            turn(128 - TURN[0] - TURN[1])
+            turn(128 - 56)
 
     star_gather(sc, group, base, send, x2, y2, along, across, idle)
-    total = grads[pl.ds(pl.multiple_of(z * 64, 64), 64), :]
+    total = grads[pl.ds(pl.multiple_of(z * 64, 64), 64), :].astype(F32)
     for e in range(1, 8):
         slices[e - 1].wait_recv()
-        total = total + gr[e]
+        total = total + gr[e].astype(F32)
     gsum[...] = total
     stay.wait()
     for cp in sent:
@@ -527,8 +543,8 @@
             pltpu.VMEM((8, 8, 128), F32),
             pltpu.VMEM((ND, 128), F32),
             pltpu.VMEM((ND, 128), BF),
-            pltpu.VMEM((512, 128), F32),
-            pltpu.VMEM((8, 64, 128), F32),
+            pltpu.VMEM((512, 128), BF),
+            pltpu.VMEM((8, 64, 128), BF),
             pltpu.SemaphoreType.DMA((60,)),
             pltpu.SemaphoreType.DMA((3, 3)),
             pltpu.SemaphoreType.DMA((5,)),
@@ -624,8 +640,7 @@
     cross(7)
     cross(0)
     halves.wait_recv()
-    total = gpart[pl.ds(pl.multiple_of(k * 32, 32), 32), :] + gk[...]
-    gsrc[0] = total
+    gsrc[0] = gpart[pl.ds(pl.multiple_of(k * 32, 32), 32), :] + gk[...]
     swaps = [send(gsrc.at[0], gx.at[i], q1.at[i], xpeers[i]) for i in range(3)]
     for part in (2, 0, 1):
         for d in range(2):
@@ -633,8 +648,7 @@
     gx[3] = gsrc[0]
     for cp in swaps:
         cp.wait_recv()
-    total = in_order(gx, xx, 4)
-    gsrc[1] = total
+    gsrc[1] = in_order(gx, xx, 4)
     swaps = [send(gsrc.at[1], gy.at[i], q2.at[i], ypeers[i]) for i in range(3)]
     for part in (2, 0, 1):
         for d in range(2):
@@ -643,7 +657,7 @@
         cp.wait_recv()
     total = (gsrc[1] + gy[0]) + (gy[1] + gy[2])
     mine_at = gall.at[z, k]
-    gall[z, k] = total
+    gall[z, k] = total.astype(BF)
     swaps = [send(mine_at, mine_at, q3.at[i], zpeers[i]) for i in range(7)]
     for part in (2, 0, 1):
         for d in range(2):
@@ -661,7 +675,7 @@
     for i, ref in enumerate((grad_self, grad_neigh)):
         for h in range(2):
             lo = i * 4 + h * 2
-            ref[:, h * 128 : h * 128 + 128] = gall[lo : lo + 2].reshape(128, 128)
+            ref[:, h * 128 : h * 128 + 128] = gall[lo : lo + 2].astype(F32).reshape(128, 128)
     for cp in sent:
         cp.wait_send()
 
@@ -688,7 +702,7 @@
             pltpu.VMEM((4, 32, 128), F32),
             pltpu.VMEM((3, 32, 128), F32),
             pltpu.VMEM((2, 32, 128), F32),
-            pltpu.VMEM((8, 2, 32, 128), F32),
+            pltpu.VMEM((8, 2, 32, 128), BF),
             pltpu.SemaphoreType.DMA((90,)),
             pltpu.SemaphoreType.DMA((2, 4, 3)),
             pltpu.SemaphoreType.DMA((9,)),

time: 106 us -> 102 us (0.962)
  Pallas kernels: 104 us -> 100 us
    pallas_call x1, Pallas kernels: 32.1 us -> 30.1 us  [node(): pl.pallas_call(node_kernel, out_shape=[jax.ShapeDtypeStruct((ND, 256), BF...]
where the time goes in v4:
time: 102 us
  Pallas kernels  100 us (98%)
  between operations  1.43 us (1%)
    pallas_call x1, Pallas kernels, scatter_rows(): pl.pallas_call(scatter_kernel, out_shape=[jax.ShapeDtypeStruct((ND, 128),...  33.9 us
    pallas_call x1, Pallas kernels, gather_rows(): pl.pallas_call(gather_kernel, out_shape=[jax.ShapeDtypeStruct((32 * ND, 1...  31.2 us
    pallas_call x1, Pallas kernels, node(): pl.pallas_call(node_kernel, out_shape=[jax.ShapeDtypeStruct((ND, 256), BF...  30.1 us
    pallas_call x1, Pallas kernels, backward(): pl.pallas_call(backward_kernel, out_shape=[jax.ShapeDtypeStruct((32 * ND,...  2.57 us

profile of v4, /device:TPU:1, one launch (start us, length us, event | category | flops | bytes accessed | tf_op | source)
XLA Modules:
  0.0 101.8 jit_solution(10553169999078580062)
XLA Ops:
  1.3 0.0 copy-start.4
  1.3 0.0 copy-start.5
  1.3 31.2 %gather_rows.1 = (bf16[16384,128]{1,0:T(8,128)(2,1)S(1)}, bf16[128,128,128]{2,1,0:T(8,128)(2,1)S(1)}, f32[64,128]{1,0:T(8,128)S(1)}) custom-call(s32[1]{0:T(128)} %bitcast.7.cnt, s32[1,512]{1,0:T(1,128)} %bitcast.11, bf16[512,128]{1,0:T(8,128)(2,1)} %x.3, s32[512,4096]{1,0:T(8,128)} %bitcast.17), custom_call_target="tpu_custom_call" | custom-call | tf_op jit(solution)/shard_map/gather_rows/pallas_call | solution.py:278
  32.5 0.0 copy-done.4
  32.5 0.0 copy-done.5
  32.5 0.0 copy-start
  32.5 0.0 copy-start.1
  32.5 0.0 copy-start.2
  32.6 0.0 copy-start.3
  32.6 0.0 copy-start.6
  32.6 1.8 %forward.1.raw_part = bf16[4096,128]{1,0:T(8,128)(2,1)S(1)} custom-call(s32[1]{0:T(128)} %bitcast.8.cnt, s32[512]{0:T(512)S(1)} %bitcast.14, s32[512]{0:T(512)S(1)} %bitcast.12, bf16[128,128,128]{2,1,0:T(8,128)(2,1)S(1)} %get-tuple-element.20.blocks.zf, bf16[16384,128]{1,0:T(8,128)(2,1)S(1)} %get-tuple-element.21.table), custom_call_target="tpu_custom_call" | custom-call | tf_op jit(solution)/shard_map/forward/pallas_call | solution.py:339
  34.4 0.0 copy-done
  34.4 0.0 copy-done.1
  34.5 0.0 copy-done.2
  34.5 0.0 copy-done.3
  34.5 0.0 copy-done.6
  34.5 30.1 %node.1 = (bf16[512,256]{1,0:T(8,128)(2,1)S(1)}, bf16[4096,128]{1,0:T(8,128)(2,1)S(1)}, f32[512,128]{1,0:T(8,128)S(1)}, f32[64,128]{1,0:T(8,128)S(1)}, bf16[128,128,128]{2,1,0:T(8,128)(2,1)S(1)}) custom-call(bf16[4096,128]{1,0:T(8,128)(2,1)S(1)} %forward.1.raw_part, f32[64,128]{1,0:T(8,128)S(1)} %get-tuple-element.22.deg, bf16[512,128]{1,0:T(8,128)(2,1)S(1)} %copy-done, ...), custom_call_target="tpu_custom_call" | custom-call | tf_op jit(solution)/shard_map/node/pallas_call | solution.py:526
  64.6 2.6 %backward.1 = (bf16[16384,128]{1,0:T(8,128)(2,1)S(1)}, bf16[512,256]{1,0:T(8,128)(2,1)}) custom-call(s32[1]{0:T(128)} %bitcast.9.cnt, s32[512]{0:T(512)S(1)} %bitcast.13, s32[512]{0:T(512)S(1)} %bitcast.15, bf16[128,128,128]{2,1,0:T(8,128)(2,1)S(1)} %get-tuple-element.23.blocks, bf16[4096,128]{1,0:T(8,128)(2,1)S(1)} %get-tuple-element.24.table, ...), custom_call_target="tpu_custom_call" | custom-call | tf_op jit(solution)/shard_map/backward/pallas_call | solution.py:358
  67.2 33.9 %scatter_rows.1 = (bf16[512,128]{1,0:T(8,128)(2,1)S(1)}, f32[128,256]{1,0:T(8,128)S(1)}, f32[128,256]{1,0:T(8,128)S(1)}) custom-call(bf16[8,2,2,512,128]{4,3,2,1,0:T(8,128)(2,1)S(1)} %bitcast.10, f32[512,128]{1,0:T(8,128)S(1)} %get-tuple-element.28.own_term, f32[64,128]{1,0:T(8,128)S(1)} %get-tuple-element.29.gpart), custom_call_target="tpu_custom_call" | custom-call | tf_op jit(solution)/shard_map/scatter_rows/pallas_call | solution.py:684
  101.1 0.8 finish.1
Async XLA Ops:
  1.3 31.2 %copy-start.4 = (s32[1,1,512]{2,1,0:T(1,128)S(1)}, s32[1,1,512]{2,1,0:T(1,128)}, u32[]{:S(2)}) copy-start(s32[1,1,512]{2,1,0:T(1,128)} %param.12) | copy-start | bytes 6148
  1.3 31.2 %copy-start.5 = (s32[1,1,512]{2,1,0:T(1,128)S(1)}, s32[1,1,512]{2,1,0:T(1,128)}, u32[]{:S(2)}) copy-start(s32[1,1,512]{2,1,0:T(1,128)} %param.13) | copy-start | bytes 6148
  32.5 1.9 %copy-start = (bf16[512,128]{1,0:T(8,128)(2,1)S(1)}, bf16[512,128]{1,0:T(8,128)(2,1)}, u32[]{:S(2)}) copy-start(bf16[512,128]{1,0:T(8,128)(2,1)} %x.3) | copy-start | bytes 393220
  32.5 1.9 %copy-start.1 = (bf16[512,256]{1,0:T(8,128)(2,1)S(1)}, bf16[512,256]{1,0:T(8,128)(2,1)}, u32[]{:S(2)}) copy-start(bf16[512,256]{1,0:T(8,128)(2,1)} %cot.1) | copy-start | bytes 786436
  32.5 1.9 %copy-start.2 = (bf16[128,256]{1,0:T(8,128)(2,1)S(1)}, bf16[128,256]{1,0:T(8,128)(2,1)}, u32[]{:S(2)}) copy-start(bf16[128,256]{1,0:T(8,128)(2,1)} %ws.1) | copy-start | bytes 196612
  32.6 1.9 %copy-start.3 = (bf16[128,256]{1,0:T(8,128)(2,1)S(1)}, bf16[128,256]{1,0:T(8,128)(2,1)}, u32[]{:S(2)}) copy-start(bf16[128,256]{1,0:T(8,128)(2,1)} %wn.1) | copy-start | bytes 196612
  32.6 1.9 %copy-start.6 = (s32[512]{0:T(512)S(1)}, s32[512]{0:T(512)}, u32[]{:S(2)}) copy-start(s32[512]{0:T(512)} %param.16) | copy-start | bytes 6148

commit v5 on v4

--- a/solution.py
+++ b/solution.py
@@ -433,11 +433,22 @@
             total = total + rx[e - 1, part].astype(F32)
         return total
 
+    turned = [0]
+
+    def turn(n):
+        lo = turned[0]
+        turned[0] += n
+
+        @pl.loop(lo, lo + n)
+        def _(i):
+            zt[i] = zf[i].T
+
     pass_on(2)
     pass_on(1)
     pass_on(3)
     fsrc[...] = final(2, mine(0, 1, 0)[...].astype(F32)).astype(BF)
     last = send(fsrc, fy, y1.at[4], across)
+    turn(32)
     rd[0] = deg[pl.ds(pl.multiple_of(col * 8, 8), 8), :]
     keep = early[0]
     for cp in degs:
@@ -482,16 +493,6 @@
             src = grads.at[pl.ds(pl.multiple_of(zat[e] * 64, 64), 64)]
             slices.append(send(src, gr.at[e], gsem.at[e], (zat[e] * 4 + side, col)))
 
-    turned = [0]
-
-    def turn(n):
-        lo = turned[0]
-        turned[0] += n
-
-        @pl.loop(lo, lo + n)
-        def _(i):
-            zt[i] = zf[i].T
-
     stay = pltpu.make_async_copy(sc, group.at[pl.ds(base(0, 0), ND)], ls)
 
     def idle(when):
@@ -509,7 +510,7 @@
             turn(8)
         else:
             later()
-            turn(128 - 56)
+            turn(128 - 88)
 
     star_gather(sc, group, base, send, x2, y2, along, across, idle)
     total = grads[pl.ds(pl.multiple_of(z * 64, 64), 64), :].astype(F32)

time: 102 us -> 101 us (level)
    pallas_call x1, Pallas kernels: 33.9 us -> 32.2 us  [scatter_rows(): pl.pallas_call(scatter_kernel, out_shape=[jax.ShapeDtypeStruct((ND, 128),...]
    pallas_call x1, Pallas kernels: 30.1 us -> 31.3 us  [node(): pl.pallas_call(node_kernel, out_shape=[jax.ShapeDtypeStruct((ND, 256), BF...]
where the time goes in v5:
time: 101 us
  Pallas kernels  99.9 us (99%)
  between operations  1.43 us (1%)
    pallas_call x1, Pallas kernels, scatter_rows(): pl.pallas_call(scatter_kernel, out_shape=[jax.ShapeDtypeStruct((ND, 128),...  32.2 us
    pallas_call x1, Pallas kernels, node(): pl.pallas_call(node_kernel, out_shape=[jax.ShapeDtypeStruct((ND, 256), BF...  31.3 us
    pallas_call x1, Pallas kernels, gather_rows(): pl.pallas_call(gather_kernel, out_shape=[jax.ShapeDtypeStruct((32 * ND, 1...  31.2 us
    pallas_call x1, Pallas kernels, backward(): pl.pallas_call(backward_kernel, out_shape=[jax.ShapeDtypeStruct((32 * ND,...  2.57 us

profile of v5, /device:TPU:1, one launch (start us, length us, event | category | flops | bytes accessed | tf_op | source)
XLA Modules:
  0.0 101.4 jit_solution(10014938408212160687)
XLA Ops:
  1.3 0.0 copy-start.4
  1.3 0.0 copy-start.5
  1.3 31.2 %gather_rows.1 = (bf16[16384,128]{1,0:T(8,128)(2,1)S(1)}, bf16[128,128,128]{2,1,0:T(8,128)(2,1)S(1)}, f32[64,128]{1,0:T(8,128)S(1)}) custom-call(s32[1]{0:T(128)} %bitcast.7.cnt, s32[1,512]{1,0:T(1,128)} %bitcast.11, bf16[512,128]{1,0:T(8,128)(2,1)} %x.3, s32[512,4096]{1,0:T(8,128)} %bitcast.17), custom_call_target="tpu_custom_call" | custom-call | tf_op jit(solution)/shard_map/gather_rows/pallas_call | solution.py:278
  32.5 0.0 copy-done.4
  32.5 0.0 copy-done.5
  32.5 0.0 copy-start
  32.5 0.0 copy-start.1
  32.5 0.0 copy-start.2
  32.6 0.0 copy-start.3
  32.6 0.0 copy-start.6
  32.6 1.8 %forward.1.raw_part = bf16[4096,128]{1,0:T(8,128)(2,1)S(1)} custom-call(s32[1]{0:T(128)} %bitcast.8.cnt, s32[512]{0:T(512)S(1)} %bitcast.14, s32[512]{0:T(512)S(1)} %bitcast.12, bf16[128,128,128]{2,1,0:T(8,128)(2,1)S(1)} %get-tuple-element.20.blocks.zf, bf16[16384,128]{1,0:T(8,128)(2,1)S(1)} %get-tuple-element.21.table), custom_call_target="tpu_custom_call" | custom-call | tf_op jit(solution)/shard_map/forward/pallas_call | solution.py:339
  34.4 0.0 copy-done
  34.4 0.0 copy-done.1
  34.5 0.0 copy-done.2
  34.5 0.0 copy-done.3
  34.5 0.0 copy-done.6
  34.5 31.3 %node.1 = (bf16[512,256]{1,0:T(8,128)(2,1)S(1)}, bf16[4096,128]{1,0:T(8,128)(2,1)S(1)}, f32[512,128]{1,0:T(8,128)S(1)}, f32[64,128]{1,0:T(8,128)S(1)}, bf16[128,128,128]{2,1,0:T(8,128)(2,1)S(1)}) custom-call(bf16[4096,128]{1,0:T(8,128)(2,1)S(1)} %forward.1.raw_part, f32[64,128]{1,0:T(8,128)S(1)} %get-tuple-element.22.deg, bf16[512,128]{1,0:T(8,128)(2,1)S(1)} %copy-done, ...), custom_call_target="tpu_custom_call" | custom-call | tf_op jit(solution)/shard_map/node/pallas_call | solution.py:527
  65.8 2.6 %backward.1 = (bf16[16384,128]{1,0:T(8,128)(2,1)S(1)}, bf16[512,256]{1,0:T(8,128)(2,1)}) custom-call(s32[1]{0:T(128)} %bitcast.9.cnt, s32[512]{0:T(512)S(1)} %bitcast.13, s32[512]{0:T(512)S(1)} %bitcast.15, bf16[128,128,128]{2,1,0:T(8,128)(2,1)S(1)} %get-tuple-element.23.blocks, bf16[4096,128]{1,0:T(8,128)(2,1)S(1)} %get-tuple-element.24.table, ...), custom_call_target="tpu_custom_call" | custom-call | tf_op jit(solution)/shard_map/backward/pallas_call | solution.py:358
  68.4 32.2 %scatter_rows.1 = (bf16[512,128]{1,0:T(8,128)(2,1)S(1)}, f32[128,256]{1,0:T(8,128)S(1)}, f32[128,256]{1,0:T(8,128)S(1)}) custom-call(bf16[8,2,2,512,128]{4,3,2,1,0:T(8,128)(2,1)S(1)} %bitcast.10, f32[512,128]{1,0:T(8,128)S(1)} %get-tuple-element.28.own_term, f32[64,128]{1,0:T(8,128)S(1)} %get-tuple-element.29.gpart), custom_call_target="tpu_custom_call" | custom-call | tf_op jit(solution)/shard_map/scatter_rows/pallas_call | solution.py:685
  100.6 0.8 finish.1
Async XLA Ops:
  1.3 31.2 %copy-start.4 = (s32[1,1,512]{2,1,0:T(1,128)S(1)}, s32[1,1,512]{2,1,0:T(1,128)}, u32[]{:S(2)}) copy-start(s32[1,1,512]{2,1,0:T(1,128)} %param.12) | copy-start | bytes 6148
  1.3 31.2 %copy-start.5 = (s32[1,1,512]{2,1,0:T(1,128)S(1)}, s32[1,1,512]{2,1,0:T(1,128)}, u32[]{:S(2)}) copy-start(s32[1,1,512]{2,1,0:T(1,128)} %param.13) | copy-start | bytes 6148
  32.5 1.9 %copy-start = (bf16[512,128]{1,0:T(8,128)(2,1)S(1)}, bf16[512,128]{1,0:T(8,128)(2,1)}, u32[]{:S(2)}) copy-start(bf16[512,128]{1,0:T(8,128)(2,1)} %x.3) | copy-start | bytes 393220
  32.5 1.9 %copy-start.1 = (bf16[512,256]{1,0:T(8,128)(2,1)S(1)}, bf16[512,256]{1,0:T(8,128)(2,1)}, u32[]{:S(2)}) copy-start(bf16[512,256]{1,0:T(8,128)(2,1)} %cot.1) | copy-start | bytes 786436
  32.5 1.9 %copy-start.2 = (bf16[128,256]{1,0:T(8,128)(2,1)S(1)}, bf16[128,256]{1,0:T(8,128)(2,1)}, u32[]{:S(2)}) copy-start(bf16[128,256]{1,0:T(8,128)(2,1)} %ws.1) | copy-start | bytes 196612
  32.6 1.9 %copy-start.3 = (bf16[128,256]{1,0:T(8,128)(2,1)S(1)}, bf16[128,256]{1,0:T(8,128)(2,1)}, u32[]{:S(2)}) copy-start(bf16[128,256]{1,0:T(8,128)(2,1)} %wn.1) | copy-start | bytes 196612
  32.6 1.9 %copy-start.6 = (s32[512]{0:T(512)S(1)}, s32[512]{0:T(512)}, u32[]{:S(2)}) copy-start(s32[512]{0:T(512)} %param.16) | copy-start | bytes 6148
